TPU v7x, 32 devices: a whole 2x2x4 slice. The times are simulated.
32 devices in a mesh: row: 4 (over y, x), col: 8 (over z, core).
Axes of the slice: x: 2, y: 2, z: 4, core: 2. Of those that a mesh axis runs over, the one named last changes fastest.
Arguments:
- local_ops: bfloat16 [4, 8, 2048, 2048], P('row', 'col'), may hold values from -2 to 30, as said below
- loads: float32 [4, 8, 2048, 256], P('row', 'col'), may hold values from -6 to 6
- modes: float32 [4, 8, 32, 2048], P('row', 'col'), may hold values from -1 to 1
- coarse_inverse: float32 [1024, 1024], P('row', 'col'), may hold values from -1 to 1
- face_rows: int32 [4, 8, 4, 512], P('row', 'col'), may hold values from 0 to 2047, as said below
- adjacency: int32 [4, 8, 4], P('row', 'col'), may hold values from 0 to 1, as said below
- contact: int32 [4, 8, 2048], P('row', 'col'), may hold values 0 or 1
Outputs:
- multipliers: float32 [4, 8, 2048, 256], P('row', 'col')
Inputs may be any that keep to these rules, and one draw needn't show every extreme that they name: `face_rows`: for each subdomain the 2048 entries are a permutation of 0 to 2047. `adjacency`: symmetric across each shared face (a subdomain's south flag equals the north flag of the one below it, its east flag the west flag of the one to its right); 0 on faces at the grid's edge. `local_ops`: each subdomain's local dual operator is symmetric positive definite.
All inputs are finite; a program needn't handle non-finite values. No bound on the sum of `contact` on one device may be relied on, other than what follows from the above.
Results may differ from a plain program's by a relative error of at most 0.00099.
Values sent between devices are 32-bit elements; how exact they have to be, the bound alone decides.
No kernel may reach another device: no remote copies, remote signals or barrier semaphores. Data moves between devices by JAX's collectives and lax.ppermute only.
A program may use at most 128 MiB of HBM per device.

v0:
```python
import functools

import jax
import jax.numpy as jnp
from jax import lax
from jax.experimental import pallas as pl
from jax.experimental.pallas import tpu as pltpu
from jax.sharding import PartitionSpec as P

F32 = jnp.float32
BF16 = jnp.bfloat16
PAD = 8
GRANT = 8 * 1024 * 1024
UNROLL = dict(add=1, extend=1, prepare=1, first=2, sums=2)
LIGHT = ("step_sums", "add")
VMEM = pl.BlockSpec(memory_space=pltpu.VMEM)
SMEM = pl.BlockSpec(memory_space=pltpu.SMEM)
HBM = pl.BlockSpec(memory_space=pltpu.HBM)


def dot(a, b):
    return lax.dot_general(a, b, (((1,), (0,)), ((), ())), preferred_element_type=F32)


def dot_nt(a, b):
    return lax.dot_general(a, b, (((1,), (1,)), ((), ())), preferred_element_type=F32)


def parts_of(x):
    high = x.astype(BF16)
    return high, (x - high.astype(F32)).astype(BF16)


def dot3(a, b):
    return dot(a[0], b[0]) + (dot(a[0], b[1]) + dot(a[1], b[0]))


def column_of(row, lanes=128):
    return jnp.transpose(jnp.broadcast_to(row, (lanes, row.shape[1])))[:, :1]


def over_tiles(order, tile, unroll, body):
    @pl.loop(0, order // tile, unroll=unroll)
    def _(i):
        begin = pl.multiple_of(i * tile, tile)
        body(begin, pl.ds(begin, tile))


def total_of(refs):
    value = refs[0][...]
    for ref in refs[1:]:
        value = value + ref[...]
    return value


def call(kernel, name, args, in_specs, outs, scratch, flops, aliases=None):
    moved = sum(x.size * x.dtype.itemsize for x in args)
    if name in LIGHT:
        flops, moved = flops // 100, moved // 100
    return pl.pallas_call(
        kernel,
        in_specs=in_specs,
        out_specs=[VMEM] * len(outs),
        out_shape=outs,
        scratch_shapes=scratch,
        compiler_params=pltpu.CompilerParams(vmem_limit_bytes=GRANT),
        cost_estimate=pl.CostEstimate(flops=int(flops), bytes_accessed=int(moved), transcendentals=0),
        input_output_aliases=aliases or {},
        name=name,
    )(*args)


def in_hbm(x):
    return pltpu.with_memory_space_constraint(x, pltpu.HBM)


def in_vmem(arrays):
    return [pltpu.with_memory_space_constraint(x, pltpu.VMEM) for x in arrays]


def shaped(shape, dtype=F32):
    return pltpu.VMEM(shape, dtype)


def pair_face(base, index):
    return base + 1 - index % 2


def cross_face(base, index):
    return base + index % 2


def splits(grid_rows):
    return grid_rows if grid_rows == 4 else 0


def has_cross(index, size):
    return jnp.logical_and(index > 0, index < size - 1)


def face_kernel(base, with_modes, split, place_ref, *refs):
    if base:
        rows_ref, x_parts, *refs = refs
        if with_modes:
            m_parts, *refs = refs
        outs = refs
    elif with_modes:
        sources, refs = refs[:4], refs[4:]
        *outs, x_parts, m_parts, rows_ref, three_ref, x_ref, modes_ref, tile_ref, sems = refs
        copies = [
            pltpu.make_async_copy(source, held, sems.at[k])
            for k, (source, held) in enumerate(zip(sources, (rows_ref, x_ref, modes_ref, tile_ref)))
        ]
        for copy in copies:
            copy.start()
        for copy in copies:
            copy.wait()
        high, low = parts_of(modes_ref[...])
        count = modes_ref.shape[0]
        m_parts[:count] = high
        m_parts[count:] = low
        size = three_ref.shape[0]
        for c in range(size):
            for k in range(3):
                begin = (c + k - 1) % size * count
                three_ref[c, k * count : (k + 1) * count] = tile_ref[begin : begin + count]
    else:
        rows_ref, x_ref, *outs, x_parts = refs
    order, cases = x_parts.shape[0], x_parts.shape[1] // 2
    if not base:
        high, low = parts_of(x_ref[...])
        x_parts[:, :cases] = high
        x_parts[:, cases:] = low
    count = m_parts.shape[0] // 2 if with_modes else 0
    index = place_ref[base // 2]
    half = rows_ref.shape[1] // 2
    chunks = half // cases
    lanes = lax.broadcasted_iota(jnp.int32, (half, order), 1)
    tall = half + chunks * count
    pair, cross = pair_face(base, index), cross_face(base, index)
    places = [(outs[0], 0, pair, 0), (outs[0], tall, pair, 1), (outs[1], 0, cross, 0), (outs[1], tall, cross, 1)]
    if split:
        inner = has_cross(index, split)
        both_ref, other_ref, last_ref = outs[:3]
        places = [
            (both_ref, 0, jnp.where(inner, cross, pair), 0),
            (both_ref, tall, pair, jnp.where(inner, 0, 1)),
            (other_ref, 0, cross, 1),
            (last_ref, 0, pair, 1),
        ]
    for target, at, face, b in places:
        if isinstance(b, int):
            row = rows_ref[pl.ds(face, 1), b * half : (b + 1) * half]
        else:
            row = jnp.where(b == 0, rows_ref[pl.ds(face, 1), :half], rows_ref[pl.ds(face, 1), half:])
        picked = jnp.where(column_of(row) == lanes, 1.0, 0.0).astype(BF16)
        got = dot(picked, x_parts[...])
        target[at : at + half] = got[:, :cases] + got[:, cases:]
        if with_modes:
            got = dot_nt(m_parts[...], picked)
            got = got[:count] + got[count:]
            for c in range(chunks):
                begin = at + half + c * count
                target[begin : begin + count] = got[:, c * cases : (c + 1) * cases]


def to_faces(base, place, rows, x, modes=None, tile_block=None):
    order, cases = x.shape[0], x.shape[1] // (2 if base else 1)
    half = rows.shape[1] // 2
    tall = half
    args, scratch = [place, rows, x], []
    if modes is not None:
        count = modes.shape[0] // (2 if base else 1)
        tall += half // cases * count
        args = [place, rows, x, modes]
    whole, part = shaped((2 * tall, cases)), shaped((tall, cases))
    split = 0 if base else splits(lax.axis_size("row"))
    outs = [whole, part, part] if split else [whole, whole]
    if not base:
        outs.append(shaped((order, 2 * cases), BF16))
        if modes is not None:
            args = [place] + [in_hbm(arg) for arg in (rows, x, modes, tile_block)]
            outs += [shaped((2 * count, order), BF16), shaped(rows.shape, rows.dtype)]
            outs.append(shaped((tile_block.shape[0] // count, 3 * count, tile_block.shape[1])))
            scratch = [pltpu.VMEM(arg.shape, F32) for arg in (x, modes, tile_block)]
            scratch.append(pltpu.SemaphoreType.DMA((4,)))
    return call(
        functools.partial(face_kernel, base, modes is not None, split),
        ("row" if base == 0 else "col") + "_faces",
        args,
        [SMEM] + [HBM if scratch else VMEM] * (len(args) - 1),
        outs,
        scratch,
        2 * order * order * cases,
    )


def faces_of(kinds, place_ref):
    return [(cross_face if cross else pair_face)(base, place_ref[base // 2]) for base, cross in kinds]


def halves_of(blocks, tall, index):
    if len(blocks) == 3:
        both, last, other = (block[...] for block in blocks)
        inner = has_cross(index, 4)
        second = jnp.where(inner, both[tall:], last)
        return [(jnp.where(inner, both[:tall], both[tall:]), second), (other, last)]
    return [(block[:tall], block[tall:]) for block in blocks]


def take_blocks(faces, adj_ref, blocks, index, half, count, r_parts, m_parts):
    cases = blocks[0].shape[1]
    chunks = half // cases
    tall = half + chunks * count
    if count:
        m_parts[...] = jnp.zeros_like(m_parts)
    for k, (face, halves) in enumerate(zip(faces, halves_of(blocks, tall, index))):
        glued = adj_ref[face].astype(F32)
        for b, source in enumerate(halves):
            high, low = parts_of(source[:half] * glued)
            begin = (2 * k + b) * half
            r_parts[begin : begin + half, :cases] = high
            r_parts[begin : begin + half, cases:] = low
            for c in range(chunks if count else 0):
                modes = half + c * count
                both = parts_of(jnp.transpose(source[modes : modes + count] * glued))
                rows = slice(begin + c * cases, begin + (c + 1) * cases)
                m_parts[rows, 2 * k * count : 2 * (k + 1) * count] = jnp.concatenate(both, axis=1)


def placed_rows(faces, rows_ref, begin, tile):
    ids = lax.broadcasted_iota(jnp.int32, (tile, rows_ref.shape[1]), 0) + begin
    return [jnp.where(rows_ref[pl.ds(face, 1), :] == ids, 1.0, 0.0) for face in faces]


def add_kernel(kinds, n_blocks, first, last, extra, count, tile, place_ref, adj_ref, rows_ref, x_ref, *refs):
    refs = list(refs)
    modes_ref = refs.pop(0) if last else None
    sums_ref = refs.pop(0) if extra else None
    blocks = [refs.pop(0) for _ in range(n_blocks)]
    out_ref = refs.pop(0)
    coef_ref = refs.pop(0) if last else None
    m_parts = refs.pop(0) if count else None
    r_parts = refs.pop(0)
    if first:
        copy = pltpu.make_async_copy(x_ref, out_ref, refs.pop(0))
        copy.start()
    order, cases = out_ref.shape
    faces = faces_of(kinds, place_ref)
    take_blocks(faces, adj_ref, blocks, place_ref[0], rows_ref.shape[1] // 2, count, r_parts, m_parts)
    if first:
        copy.wait()
        x_ref = out_ref
    sign = -1.0 if count and last else 1.0

    def body(begin, rows):
        ones = placed_rows(faces, rows_ref, begin, tile)
        total = dot(jnp.concatenate([one.astype(BF16) for one in ones], axis=1), r_parts[...])
        out_ref[rows] = sign * (x_ref[rows] + (total[:, :cases] + total[:, cases:]))

    over_tiles(order, tile, UNROLL["add"], body)
    if last:
        coef_ref[: modes_ref.shape[0]] = dot3(parts_of(modes_ref[...]), parts_of(out_ref[...]))
    if extra:
        coef_ref[modes_ref.shape[0] :] = sums_ref[...]


def add_faces(kinds, place, adj, rows, x, blocks, modes=None, sums=None, first=False, count=0, tile=512):
    order, cases = x.shape
    last, extra = modes is not None, sums is not None
    args = [place, adj, rows, in_hbm(x) if first else x] + [modes] * last + [sums] * extra
    args += in_vmem(blocks)
    specs = [VMEM] * len(args)
    specs[:2] = [SMEM, SMEM]
    specs[3] = HBM if first else VMEM
    outs = [shaped((order, cases))]
    if last:
        outs.append(shaped((modes.shape[0] + PAD * extra, cases)))
    if count:
        outs.append(shaped((len(kinds) * rows.shape[1], 2 * len(kinds) * count), BF16))
    scratch = [pltpu.VMEM((len(kinds) * rows.shape[1], 2 * cases), BF16)]
    if first:
        scratch.append(pltpu.SemaphoreType.DMA(()))
    return call(
        functools.partial(add_kernel, kinds, len(blocks), first, last, extra, count, tile),
        "last_add" if last else "add",
        args,
        specs,
        outs,
        scratch,
        len(kinds) * order * order * cases,
        None if first else {3: 0},
    )


def extend_kernel(groups, tile, place_ref, adj_ref, rows_ref, contact_ref, op_ref, modes_source, *refs):
    parts, refs = refs[: len(groups)], refs[len(groups) :]
    w_high, w_low, weight_ref, clamp_ref, held, modes_ref, sems = refs
    copy = pltpu.make_async_copy(op_ref, held, sems.at[0])
    modes_copy = pltpu.make_async_copy(modes_source, modes_ref, sems.at[1])
    modes_copy.start()
    copy.start()
    modes_copy.wait()
    count = modes_ref.shape[0]

    def body(begin, rows):
        glued = jnp.zeros((tile, 1), F32)
        blocks = [jnp.transpose(modes_ref[:, rows])]
        for kinds, part in zip(groups, parts):
            faces = faces_of(kinds, place_ref)
            ones = placed_rows(faces, rows_ref, begin, tile)
            for face, one in zip(faces, ones):
                glued += adj_ref[face].astype(F32) * jnp.sum(one, axis=1, keepdims=True)
            near = dot(jnp.concatenate([one.astype(BF16) for one in ones], axis=1), part[...])
            for k in range(len(faces)):
                lane = 2 * k * count
                blocks.append(near[:, lane : lane + count] + near[:, lane + count : lane + 2 * count])
        row_free = 1.0 - glued
        weight_ref[rows] = 0.5 + 0.5 * row_free
        contact = column_of(contact_ref[:, rows].astype(F32))
        clamp_ref[rows] = jnp.where(contact * row_free > 0.5, 1.0, 0.0)
        high, low = parts_of(jnp.concatenate(blocks, axis=1))
        w_high[rows] = high
        w_low[rows] = low

    over_tiles(held.shape[0], tile, UNROLL["extend"], body)
    copy.wait()


def extend(groups, place, adj, rows, contact, op, modes, parts, tile=256):
    order, count = op.shape[0], modes.shape[0]
    args = [place, adj, rows, contact, in_hbm(op), in_hbm(modes), *parts]
    w, column = shaped((order, 5 * count), BF16), shaped((order, 1))
    return call(
        functools.partial(extend_kernel, groups, tile),
        "extend",
        args,
        [SMEM, SMEM, VMEM, VMEM, HBM, HBM] + [VMEM] * len(parts),
        [w, w, column, column, shaped(op.shape, op.dtype)],
        [pltpu.VMEM(modes.shape, modes.dtype), pltpu.SemaphoreType.DMA((2,))],
        2 * order * order * 8 * count,
    )


def coarse_kernel(offsets, extra, grid_rows, place_ref, *refs):
    inverse_refs, refs = refs[:grid_rows], refs[grid_rows:]
    pieces = refs[: len(offsets)]
    outs = refs[len(offsets) : len(offsets) + grid_rows]
    coef, amounts = refs[len(offsets) + grid_rows :]
    row, col = place_ref[0], place_ref[1]
    count = inverse_refs[0].shape[1] // 3
    tall = count + extra
    sums = None
    for piece, inside in zip(pieces, offsets):
        for k, offset in enumerate(inside):
            begin = pl.multiple_of((col ^ offset) * count, count)
            coef[pl.ds(begin, count)] = piece[k * tall : k * tall + count]
            if extra:
                term = piece[k * tall + count : (k + 1) * tall]
                sums = term if sums is None else sums + term
    tiles = inverse_refs[0].shape[0]
    inverse = [jnp.concatenate([ref[k] for k in range(tiles)], axis=1) for ref in inverse_refs]
    inverse = parts_of(jnp.concatenate(inverse, axis=0))
    amounts[...] = dot3(inverse, parts_of(coef[...])).reshape(amounts.shape)
    odd = col % 2
    for j in range(grid_rows):
        target = row ^ j
        cross = jnp.clip(target - 1 + 2 * (target % 2), 0, grid_rows - 1) ^ row
        order = (j * 3 + 1, j * 3 + 2 - 2 * odd, j * 3 + 2 * odd, (j ^ 1) * 3 + 1, cross * 3 + 1)
        for k, source in enumerate(order):
            outs[j][k * count : (k + 1) * count] = amounts[source]
        if extra:
            outs[j][5 * count :] = sums


def coarse(place, inverse, pieces, offsets, extra):
    grid_rows = len(inverse)
    tiles, three, width = inverse[0].shape
    count = three // 3
    cases = pieces[0].shape[1]
    args = [place, *in_vmem(inverse), *in_vmem(pieces)]
    return call(
        functools.partial(coarse_kernel, offsets, extra, grid_rows),
        "coarse",
        args,
        [SMEM] + [VMEM] * (len(args) - 1),
        [shaped((5 * count + extra, cases))] * grid_rows,
        [pltpu.VMEM((tiles * width, cases), F32), pltpu.VMEM((grid_rows * 3, count, cases), F32)],
        6 * grid_rows * three * tiles * width * cases,
    )


def first_kernel(tile, op_ref, s_ref, w_high, w_low, clamp_ref, *refs):
    *part_refs, d_ref, v_ref, field = refs
    order, cases = s_ref.shape
    amount = parts_of(total_of(part_refs))


    def prepare(_, rows):
        d = s_ref[rows] - dot3((w_high[rows], w_low[rows]), amount)
        d_ref[rows] = d
        h = jnp.where(clamp_ref[rows] > 0.5, jnp.maximum(-d, 0.0), -d)
        high, low = parts_of(h)
        field[rows, :cases] = high
        field[rows, cases:] = low

    def body(_, rows):
        got = dot(op_ref[rows], field[...])
        v_ref[rows] = got[:, :cases] + got[:, cases:]

    over_tiles(order, tile, UNROLL["prepare"], prepare)
    over_tiles(order, tile, UNROLL["first"], body)


def first(op, s, w, clamp, amounts, tile=512):
    order, cases = s.shape
    args = [op, s, *w, clamp, *in_vmem(amounts)]
    return call(
        functools.partial(first_kernel, tile),
        "first",
        args,
        [VMEM] * len(args),
        [shaped((order, cases))] * 2,
        [pltpu.VMEM((order, 2 * cases), BF16)],
        4 * order * order * cases,
        {1: 0},
    )


def add_sums(sums_ref, tile, op_ref, d_ref, weight_ref, field):
    sums_ref[...] = jnp.zeros_like(sums_ref)


    def body(_, rows):
        operated = dot(op_ref[rows], field[...])
        d = d_ref[rows]
        sums_ref[0:1] += jnp.sum(weight_ref[rows] * d * d, axis=0, keepdims=True)
        sums_ref[1:2] += jnp.sum(d * operated, axis=0, keepdims=True)

    over_tiles(d_ref.shape[0], tile, UNROLL["sums"], body)


def sums_kernel(tile, op_ref, d_ref, weight_ref, sums_ref, field):
    field[...] = d_ref[...].astype(BF16)
    add_sums(sums_ref, tile, op_ref, d_ref, weight_ref, field)


def step_sums(op, d, weight, tile=512):
    order, cases = d.shape
    return call(
        functools.partial(sums_kernel, tile),
        "step_sums",
        [op, d, weight],
        [VMEM] * 3,
        [shaped((PAD, cases))],
        [pltpu.VMEM((order, cases), BF16)],
        2 * order * order * cases,
    )[0]


def second_kernel(tile, op_ref, s_ref, d0_ref, w_high, w_low, weight_ref, *refs):
    *part_refs, d_ref, sums_ref, step_ref, field = refs
    order, cases = s_ref.shape
    wide = w_high.shape[1]
    amount = total_of(part_refs)
    length = amount[wide : wide + 1] / amount[wide + 1 : wide + 2]
    step_ref[...] = jnp.broadcast_to(length, step_ref.shape)
    amount = parts_of(amount[:wide])


    def prepare(_, rows):
        q = s_ref[rows] - dot3((w_high[rows], w_low[rows]), amount)
        d = length * q + d0_ref[rows]
        d_ref[rows] = d
        field[rows] = d.astype(BF16)

    over_tiles(order, tile, UNROLL["prepare"], prepare)
    add_sums(sums_ref, tile, op_ref, d_ref, weight_ref, field)


def second(op, s, d0, w, weight, amounts, tile=512):
    order, cases = s.shape
    args = [op, s, d0, *w, weight, *in_vmem(amounts)]
    return call(
        functools.partial(second_kernel, tile),
        "second",
        args,
        [VMEM] * len(args),
        [shaped((order, cases)), shaped((PAD, cases)), shaped((PAD, cases))],
        [pltpu.VMEM((order, cases), BF16)],
        2 * order * order * cases,
        {1: 0},
    )


def finish_kernel(d0_ref, d1_ref, clamp_ref, step_ref, *refs):
    *sum_refs, out_ref = refs
    sums = total_of(sum_refs)
    low = jnp.where(clamp_ref[...] > 0.5, 0.0, -jnp.inf)
    once = jnp.maximum(-(step_ref[0:1] * d0_ref[...]), low)
    length = sums[0:1] / sums[1:2]
    out_ref[...] = jnp.maximum(once - length * d1_ref[...], low)


def finish(d0, d1, clamp, step, sums, tile=512):
    order, cases = d0.shape
    block = pl.BlockSpec((tile, cases), lambda i: (i, 0))
    small = pl.BlockSpec((PAD, cases), lambda i: (0, 0))
    return pl.pallas_call(
        finish_kernel,
        grid=(order // tile,),
        in_specs=[block, block, pl.BlockSpec((tile, 1), lambda i: (i, 0))] + [small] * (1 + len(sums)),
        out_specs=block,
        out_shape=jax.ShapeDtypeStruct((order, cases), F32),
        compiler_params=pltpu.CompilerParams(vmem_limit_bytes=GRANT),
        cost_estimate=pl.CostEstimate(flops=4 * order * cases, bytes_accessed=12 * order * cases, transcendentals=0),
        name="finish",
    )(d0, d1, clamp, step, *sums)


def send(x, axis, target):
    size = lax.axis_size(axis)
    pairs = [(i, target(i)) for i in range(size)]
    return lax.ppermute(x, axis, [(i, j) for i, j in pairs if j is not None and 0 <= j < size])


def swap(x, axis, bits):
    return send(x, axis, lambda i: i ^ bits)


def other_side(i):
    return i + 1 if i % 2 else i - 1


def row_exchange(*sends):
    size = lax.axis_size("row")
    if not splits(size):
        got = [swap(sends[0], "row", 1), send(sends[1], "row", other_side)]
        return got, got
    both, other, last = sends
    tall = other.shape[0]
    both = swap(both, "row", 1)
    other = send(other, "row", lambda i: i ^ 2 if i in (1, 2) else None)
    inner = has_cross(lax.axis_index("row"), size)
    got_last = swap(jnp.where(inner, last, other), "row", 1)
    got_other = send(both[:tall], "row", lambda i: i ^ 2 if i in (0, 3) else None)
    return [both, other], [both, got_last, got_other]


def col_exchange(pair, cross):
    return swap(pair, "col", 1), send(cross, "col", other_side)


def gather_cols(block):
    size = lax.axis_size("col")
    far = list(range(2, size, 2))
    pieces = [block] + [swap(block, "col", j) for j in far]
    held = jnp.concatenate(pieces, axis=0)
    known = [0] + far
    return pieces + [swap(held, "col", 1)], [[j] for j in known] + [[j ^ 1 for j in known]]


def coarse_amounts(place, inverse, block, extra):
    pieces, offsets = gather_cols(block)
    sends = coarse(place, inverse, pieces, offsets, extra)
    return [sends[0]] + [swap(sends[j], "row", j) for j in range(1, lax.axis_size("row"))], sends[0]


def by_row(three):
    grid_rows = lax.axis_size("row")
    tiles = three.shape[0] // grid_rows
    row = lax.axis_index("row")
    return [lax.dynamic_slice_in_dim(three, (row ^ j) * tiles, tiles, 0) for j in range(grid_rows)]


def spread_rows(picked):
    return [picked[0]] + [swap(picked[j], "row", j) for j in range(1, len(picked))]


def after(x, *others):
    return lax.optimization_barrier((x, *others))[0]


def after_all(arrays, others):
    return lax.optimization_barrier((*arrays, *others))[: len(arrays)]


COLS = ((2, False), (2, True))
ROWS = ((0, False), (0, True))


def per_device(local_ops, loads, modes, coarse_inverse, face_rows, adjacency, contact):
    op, load, mode = local_ops[0, 0], loads[0, 0], modes[0, 0]
    rows, adj = face_rows[0, 0], adjacency[0, 0]
    touch = contact[0, 0][None]
    count = mode.shape[0]
    place = jnp.stack([lax.axis_index("row"), lax.axis_index("col")]).astype(jnp.int32)

    *row_sends, x_parts, m_parts, rows, three = to_faces(0, place, rows, load, mode, coarse_inverse)
    way, row_got = row_exchange(*row_sends)
    col_sends = to_faces(2, place, rows, x_parts, m_parts)
    col_got = col_exchange(*after_all(col_sends, way))
    picked = by_row(lax.all_to_all(after(three, *col_sends), "col", 0, 0, tiled=True))
    inverse = spread_rows(picked)
    part, m_cols = add_faces(COLS, place, adj, rows, load, col_got, first=True, count=count)
    s0, coef, m_rows = add_faces(ROWS, after(place, *picked), adj, rows, part, row_got, modes=mode, count=count)
    amounts, own = coarse_amounts(place, inverse, after(coef, *inverse), 0)
    w_high, w_low, weight, clamp, op = extend(
        (COLS, ROWS), after(place, own), adj, rows, touch, op, mode, (m_cols, m_rows)
    )
    w = (w_high, w_low)
    d0, v = first(op, s0, w, clamp, amounts)

    *row_sends, x_parts = to_faces(0, place, rows, v)
    way, row_got = row_exchange(*row_sends)
    col_sends = to_faces(2, place, rows, x_parts)
    sums = step_sums(op, d0, after(weight, *col_sends))
    col_got = col_exchange(*after_all(col_sends, [*way[1:], sums]))
    (part,) = add_faces(COLS, place, adj, rows, v, col_got)
    s1, coef = add_faces(ROWS, place, adj, rows, part, row_got, mode, sums)
    amounts, _ = coarse_amounts(place, inverse, coef, PAD)
    d1, sums, step = second(op, s1, d0, w, weight, amounts)

    grid_rows, grid_cols = lax.axis_size("row"), lax.axis_size("col")
    sums = sum((swap(sums, "row", j) for j in range(1, grid_rows)), sums)
    sums = sum((swap(sums, "col", j) for j in range(2, grid_cols, 2)), sums)
    return finish(d0, d1, clamp, step, [sums, swap(sums, "col", 1)])[None, None]


def solution(mesh):
    placed = (
        P("row", "col", None, None),
        P("row", "col", None, None),
        P("row", "col", None, None),
        P("row", "col"),
        P("row", "col", None, None),
        P("row", "col", None),
        P("row", "col", None),
    )
    return jax.shard_map(
        per_device,
        mesh=mesh,
        in_specs=placed,
        out_specs=P("row", "col", None, None),
        check_vma=False,
    )
```

profile of v0, /device:TPU:0, one launch (start us, length us, event | category | flops | bytes accessed | tf_op | source)
XLA Modules:
  0.0 157.0 jit_solution(11366973105329277497)
XLA Ops:
  0.1 6.6 %row_faces.2 = (f32[576,256]{1,0:T(8,128)S(1)}, f32[288,256]{1,0:T(8,128)S(1)}, f32[288,256]{1,0:T(8,128)S(1)}, bf16[2048,512]{1,0:T(8,128)(2,1)S(1)}, bf16[64,2...) custom-call(s32[2]{0:T(128)S(1)} %pad_add_fusion.place_ref, s32[4,512]{1,0:T(4,128)} %bitcast.22, ...), custom_call_target="tpu_custom_call" | custom-call | flops 2147483648 | bytes 2498568 | tf_op jit(solution)/shard_map/row_faces/pallas_call | solution.py:60
  6.7 3.0 %collective-permute-start.3 = (f32[576,256]{1,0:T(8,128)S(1)}, f32[576,256]{1,0:T(8,128)S(1)}, u32[]{:S(2)}, u32[]{:S(2)}) collective-permute-start(f32[576,256]{1,0:T(8,128)S(1)} %get-tuple-element.62), channel_id=1, source_target_pairs={{0,8},{8,0},{16,24},{24,16},{1,9},{9,1},{17,25},{25,17},{2,10},{10... | collective-permute-start | bytes 1769480 | tf_op jit(solution)/shard_map/ppermute | solution.py:524
  11.0 4.4 %col_faces.2 = (f32[576,256]{1,0:T(8,128)S(1)}, f32[576,256]{1,0:T(8,128)S(1)}) custom-call(s32[2]{0:T(128)S(1)} %pad_add_fusion.place_ref, s32[4,512]{1,0:T(4,128)S(1)} %get-tuple-element.55.refs_0_.rows_ref, bf16[2048,512]{1,0:T(8,128)(2,1)S(1)} %get-tuple-element.56.refs_1_, bf16[64,2048]{1,0:T(8,128)(2,1)S(1)} %get-tuple-element.57.refs_2_), custom_call_target="tpu_custom_call" | custom-call | flops 2147483648 | bytes 2367496 | tf_op jit(solution)/shard_map/col_faces/pallas_call | solution.py:60
  15.4 4.9 %all-to-all-start = ((f32[8,96,128]{2,1,0:T(8,128)}), f32[8,96,128]{2,1,0:T(8,128)}, u32[]{:S(2)}, u32[]{:S(2)}) async-start(f32[8,96,128]{2,1,0:T(8,128)} %get-tuple-element.60), calls=%async_computation | async-start | bytes 786432 | tf_op jit(solution)/shard_map/all_to_all | solution.py:603
  20.3 2.7 %collective-permute-done.3.refs_1_ = f32[576,256]{1,0:T(8,128)S(1)} collective-permute-done((f32[576,256]{1,0:T(8,128)S(1)}, f32[576,256]{1,0:T(8,128)S(1)}, u32[]{:S(2)}, u32[]{:S(2)}) %collective-permute-start.3) | collective-permute-done | bytes 589856 | tf_op jit(solution)/shard_map/ppermute | solution.py:524
  27.0 4.3 %collective-permute-start.8 = (f32[288,256]{1,0:T(8,128)}, f32[288,256]{1,0:T(8,128)}, u32[]{:S(2)}, u32[]{:S(2)}) collective-permute-start(f32[288,256]{1,0:T(8,128)} %slice.8), channel_id=1, source_target_pairs={{0,16},{24,8},{1,17},{25,9},{2,18},{26,10},{3,19},{27,11},{4,20},{... | collective-permute-start | bytes 884744 | tf_op jit(solution)/shard_map/ppermute | solution.py:524
  34.2 2.7 %collective-permute-start = (f32[2,96,128]{2,1,0:T(8,128)S(1)}, f32[2,96,128]{2,1,0:T(8,128)S(1)}, u32[]{:S(2)}, u32[]{:S(2)}) collective-permute-start(f32[2,96,128]{2,1,0:T(8,128)S(1)} %get-tuple-element.105), channel_id=1, source_target_pairs={{0,8},{8,0},{16,24},{24,16},{1,9},{9,1},{17,25},{25,17},{2,10},{10... | collective-permute-start | bytes 294920 | tf_op jit(solution)/shard_map/ppermute | solution.py:524
  38.4 5.0 %add.50 = (f32[2048,256]{1,0:T(8,128)S(1)}, bf16[1024,128]{1,0:T(8,128)(2,1)S(1)}) custom-call(s32[2]{0:T(128)S(1)} %pad_add_fusion.place_ref, s32[4]{0:T(128)S(1)} %bitcast.14, s32[4,512]{1,0:T(4,128)S(1)} %get-tuple-element.55.refs_0_.rows_ref, f32[2048,256]{1,0:T(8,128)} %bitcast.21, f32[576,256]{1,0:T(8,128)S(1)} %collective-permute-done.5.refs_0_, ...), custom_call_target="tpu_custom_call" | custom-call | flops 21474836 | bytes 32850 | tf_op jit(solution)/shard_map/add/pallas_call | solution.py:60
  43.5 5.2 %last_add.2 = (f32[2048,256]{1,0:T(8,128)S(1)}, f32[32,256]{1,0:T(8,128)S(1)}, bf16[1024,128]{1,0:T(8,128)(2,1)S(1)}) custom-call(s32[2]{0:T(128)S(1)} %pad_add_fusion.place_ref, s32[4]{0:T(128)S(1)} %bitcast.15, s32[4,512]{1,0:T(4,128)S(1)} %get-tuple-element.55.refs_0_.rows_ref, ...), custom_call_target="tpu_custom_call", output_to_operand_aliasing={{0}: (3, {})} | custom-call | flops 2147483648 | bytes 3547160 | tf_op jit(solution)/shard_map/last_add/pallas_call | solution.py:60
  48.8 2.6 %collective-permute-start.10 = (f32[32,256]{1,0:T(8,128)S(1)}, f32[32,256]{1,0:T(8,128)S(1)}, u32[]{:S(2)}, u32[]{:S(2)}) collective-permute-start(f32[32,256]{1,0:T(8,128)S(1)} %get-tuple-element.69.refs_4_), channel_id=1, source_target_pairs={{0,4},{1,5},{2,6},{3,7},{4,0},{5,1},{6,2},{7,3},{8,12},{9,13},{10,... | collective-permute-start | bytes 98312 | tf_op jit(solution)/shard_map/ppermute | solution.py:524
  53.7 3.4 %collective-permute-done.11.refs_7_ = f32[32,256]{1,0:T(8,128)S(1)} collective-permute-done((f32[32,256]{1,0:T(8,128)S(1)}, f32[32,256]{1,0:T(8,128)S(1)}, u32[]{:S(2)}, u32[]{:S(2)}) %collective-permute-start.11) | collective-permute-done | bytes 32800 | tf_op jit(solution)/shard_map/ppermute | solution.py:524
  59.5 2.7 %collective-permute-start.13 = (f32[160,256]{1,0:T(8,128)S(1)}, f32[160,256]{1,0:T(8,128)S(1)}, u32[]{:S(2)}, u32[]{:S(2)}) collective-permute-start(f32[160,256]{1,0:T(8,128)S(1)} %get-tuple-element.79), channel_id=1, source_target_pairs={{0,8},{8,0},{16,24},{24,16},{1,9},{9,1},{17,25},{25,17},{2,10},{10... | collective-permute-start | bytes 491528 | tf_op jit(solution)/shard_map/ppermute | solution.py:524
  63.8 9.2 %extend.1 = (bf16[2048,160]{1,0:T(8,128)(2,1)S(1)}, bf16[2048,160]{1,0:T(8,128)(2,1)S(1)}, f32[2048,1]{1,0:T(8,128)S(1)}, f32[2048,1]{1,0:T(8,128)S(1)}, bf16[2048,2048]{1,0:T(8,128)(2,1)S(1)}) custom-call(s32[2]{0:T(128)S(1)} %pad_add_fusion.place_ref, s32[4]{0:T(128)S(1)} %bitcast.16, s32[4,512]{1,0:T(4,128)S(1)} %get-tuple-element.55.refs_0_.rows_ref, ...), custom_call_target="tpu_custom_call" | custom-call | flops 2147483648 | bytes 9191448 | tf_op jit(solution)/shard_map/extend/pallas_call | solution.py:60
  73.0 6.3 %first.1 = (f32[2048,256]{1,0:T(8,128)S(1)}, f32[2048,256]{1,0:T(8,128)S(1)}) custom-call(bf16[2048,2048]{1,0:T(8,128)(2,1)S(1)} %get-tuple-element.74.op_ref, f32[2048,256]{1,0:T(8,128)S(1)} %get-tuple-element.75.s_ref, bf16[2048,160]{1,0:T(8,128)(2,1)S(1)} %get-tuple-element.76.w_high, ...), custom_call_target="tpu_custom_call", output_to_operand_aliasing={{0}: (1, {})} | custom-call | flops 4294967296 | bytes 12460032 | tf_op jit(solution)/shard_map/first/pallas_call | solution.py:60
  79.4 3.2 %row_faces.3 = (f32[512,256]{1,0:T(8,128)S(1)}, f32[256,256]{1,0:T(8,128)S(1)}, f32[256,256]{1,0:T(8,128)S(1)}, bf16[2048,512]{1,0:T(8,128)(2,1)S(1)}) custom-call(s32[2]{0:T(128)S(1)} %pad_add_fusion.place_ref, s32[4,512]{1,0:T(4,128)S(1)} %get-tuple-element.55.refs_0_.rows_ref, f32[2048,256]{1,0:T(8,128)S(1)} %get-tuple-element.83.refs_1_.x_ref), custom_call_target="tpu_custom_call" | custom-call | flops 2147483648 | bytes 2105352 | tf_op jit(solution)/shard_map/row_faces/pallas_call | solution.py:60
  84.1 2.7 %collective-permute-start.19 = (f32[512,256]{1,0:T(8,128)S(1)}, f32[512,256]{1,0:T(8,128)S(1)}, u32[]{:S(2)}, u32[]{:S(2)}) collective-permute-start(f32[512,256]{1,0:T(8,128)S(1)} %get-tuple-element.92), channel_id=1, source_target_pairs={{0,8},{8,0},{16,24},{24,16},{1,9},{9,1},{17,25},{25,17},{2,10},{10... | collective-permute-start | bytes 1572872 | tf_op jit(solution)/shard_map/ppermute | solution.py:524
  86.8 3.0 %col_faces.3 = (f32[512,256]{1,0:T(8,128)S(1)}, f32[512,256]{1,0:T(8,128)S(1)}) custom-call(s32[2]{0:T(128)S(1)} %pad_add_fusion.place_ref, s32[4,512]{1,0:T(4,128)S(1)} %get-tuple-element.55.refs_0_.rows_ref, bf16[2048,512]{1,0:T(8,128)(2,1)S(1)} %get-tuple-element.84.refs_1_), custom_call_target="tpu_custom_call" | custom-call | flops 2147483648 | bytes 2105352 | tf_op jit(solution)/shard_map/col_faces/pallas_call | solution.py:60
  89.8 2.7 %step_sums.1.refs_1_ = f32[8,256]{1,0:T(8,128)S(1)} custom-call(bf16[2048,2048]{1,0:T(8,128)(2,1)S(1)} %get-tuple-element.74.op_ref, f32[2048,256]{1,0:T(8,128)S(1)} %get-tuple-element.82.d_ref.d0_ref, f32[2048,1]{1,0:T(8,128)S(1)} %get-tuple-element.89.weight_ref), custom_call_target="tpu_custom_call" | custom-call | flops 21474836 | bytes 104939 | tf_op jit(solution)/shard_map/step_sums/pallas_call | solution.py:60
  93.5 5.7 %collective-permute-done.19.refs_2_ = f32[512,256]{1,0:T(8,128)S(1)} collective-permute-done((f32[512,256]{1,0:T(8,128)S(1)}, f32[512,256]{1,0:T(8,128)S(1)}, u32[]{:S(2)}, u32[]{:S(2)}) %collective-permute-start.19) | collective-permute-done | bytes 524320 | tf_op jit(solution)/shard_map/ppermute | solution.py:524
  99.2 4.5 %collective-permute-start.21 = (f32[256,256]{1,0:T(8,128)S(1)}, f32[256,256]{1,0:T(8,128)S(1)}, u32[]{:S(2)}, u32[]{:S(2)}) collective-permute-start(f32[256,256]{1,0:T(8,128)S(1)} %slice.9), channel_id=1, source_target_pairs={{0,16},{24,8},{1,17},{25,9},{2,18},{26,10},{3,19},{27,11},{4,20},{... | collective-permute-start | bytes 786440 | tf_op jit(solution)/shard_map/ppermute | solution.py:524
  103.8 3.6 %add.51.x_ref = f32[2048,256]{1,0:T(8,128)S(1)} custom-call(s32[2]{0:T(128)S(1)} %pad_add_fusion.place_ref, s32[4]{0:T(128)S(1)} %bitcast.17, s32[4,512]{1,0:T(4,128)S(1)} %get-tuple-element.55.refs_0_.rows_ref, f32[2048,256]{1,0:T(8,128)S(1)} %get-tuple-element.83.refs_1_.x_ref, ...), custom_call_target="tpu_custom_call", output_to_operand_aliasing={{}: (3, {})} | custom-call | flops 21474836 | bytes 31539 | tf_op jit(solution)/shard_map/add/pallas_call | solution.py:60
  107.6 4.2 %last_add.3 = (f32[2048,256]{1,0:T(8,128)S(1)}, f32[40,256]{1,0:T(8,128)S(1)}) custom-call(s32[2]{0:T(128)S(1)} %pad_add_fusion.place_ref, s32[4]{0:T(128)S(1)} %bitcast.18, s32[4,512]{1,0:T(4,128)S(1)} %get-tuple-element.55.refs_0_.rows_ref, f32[2048,256]{1,0:T(8,128)S(1)} %add.51.x_ref, f32[32,2048]{1,0:T(8,128)S(1)} %bitcast.12, ...), custom_call_target="tpu_custom_call", output_to_operand_aliasing={{0}: (3, {})} | custom-call | flops 2147483648 | bytes 3424280 | tf_op jit(solution)/shard_map/last_add/pallas_call | solution.py:60
  111.9 2.6 %collective-permute-start.23 = (f32[40,256]{1,0:T(8,128)S(1)}, f32[40,256]{1,0:T(8,128)S(1)}, u32[]{:S(2)}, u32[]{:S(2)}) collective-permute-start(f32[40,256]{1,0:T(8,128)S(1)} %get-tuple-element.95.refs_4_), channel_id=1, source_target_pairs={{0,4},{1,5},{2,6},{3,7},{4,0},{5,1},{6,2},{7,3},{8,12},{9,13},{10,... | collective-permute-start | bytes 122888 | tf_op jit(solution)/shard_map/ppermute | solution.py:524
  117.8 2.5 %collective-permute-done.24.refs_7_ = f32[40,256]{1,0:T(8,128)S(1)} collective-permute-done((f32[40,256]{1,0:T(8,128)S(1)}, f32[40,256]{1,0:T(8,128)S(1)}, u32[]{:S(2)}, u32[]{:S(2)}) %collective-permute-start.24) | collective-permute-done | bytes 40992 | tf_op jit(solution)/shard_map/ppermute | solution.py:524
  122.7 2.6 %collective-permute-start.26 = (f32[168,256]{1,0:T(8,128)S(1)}, f32[168,256]{1,0:T(8,128)S(1)}, u32[]{:S(2)}, u32[]{:S(2)}) collective-permute-start(f32[168,256]{1,0:T(8,128)S(1)} %get-tuple-element.97), channel_id=1, source_target_pairs={{0,8},{8,0},{16,24},{24,16},{1,9},{9,1},{17,25},{25,17},{2,10},{10... | collective-permute-start | bytes 516104 | tf_op jit(solution)/shard_map/ppermute | solution.py:524
  126.8 3.6 %collective-permute-done.26.refs_1_ = f32[168,256]{1,0:T(8,128)S(1)} collective-permute-done((f32[168,256]{1,0:T(8,128)S(1)}, f32[168,256]{1,0:T(8,128)S(1)}, u32[]{:S(2)}, u32[]{:S(2)}) %collective-permute-start.26) | collective-permute-done | bytes 172064 | tf_op jit(solution)/shard_map/ppermute | solution.py:524
  130.5 4.7 %collective-permute-done.27.refs_2_ = f32[168,256]{1,0:T(8,128)S(1)} collective-permute-done((f32[168,256]{1,0:T(8,128)S(1)}, f32[168,256]{1,0:T(8,128)S(1)}, u32[]{:S(2)}, u32[]{:S(2)}) %collective-permute-start.27) | collective-permute-done | bytes 172064 | tf_op jit(solution)/shard_map/ppermute | solution.py:524
  135.1 4.2 %second.1 = (f32[2048,256]{1,0:T(8,128)S(1)}, f32[8,256]{1,0:T(8,128)S(1)}, f32[8,256]{1,0:T(8,128)S(1)}) custom-call(bf16[2048,2048]{1,0:T(8,128)(2,1)S(1)} %get-tuple-element.74.op_ref, f32[2048,256]{1,0:T(8,128)S(1)} %get-tuple-element.94.s_ref, f32[2048,256]{1,0:T(8,128)S(1)} %get-tuple-element.82.d_ref.d0_ref, ...), custom_call_target="tpu_custom_call", output_to_operand_aliasing={{0}: (1, {})} | custom-call | flops 2147483648 | bytes 14589952 | tf_op jit(solution)/shard_map/second/pallas_call | solution.py:60
  143.4 2.6 %collective-permute-done.31 = f32[8,256]{1,0:T(8,128)S(1)} collective-permute-done((f32[8,256]{1,0:T(8,128)S(1)}, f32[8,256]{1,0:T(8,128)S(1)}, u32[]{:S(2)}, u32[]{:S(2)}) %collective-permute-start.31) | collective-permute-done | bytes 8224 | tf_op jit(solution)/shard_map/ppermute | solution.py:524
  145.9 2.4 %collective-permute-start.33 = (f32[8,256]{1,0:T(8,128)S(1)}, f32[8,256]{1,0:T(8,128)S(1)}, u32[]{:S(2)}, u32[]{:S(2)}) collective-permute-start(f32[8,256]{1,0:T(8,128)S(1)} %add_add_fusion.1), channel_id=1, source_target_pairs={{0,4},{1,5},{2,6},{3,7},{4,0},{5,1},{6,2},{7,3},{8,12},{9,13},{10,... | collective-permute-start | bytes 24584 | tf_op jit(solution)/shard_map/ppermute | solution.py:524
  150.6 3.2 %collective-permute-done.34 = f32[8,256]{1,0:T(8,128)S(1)} collective-permute-done((f32[8,256]{1,0:T(8,128)S(1)}, f32[8,256]{1,0:T(8,128)S(1)}, u32[]{:S(2)}, u32[]{:S(2)}) %collective-permute-start.34) | collective-permute-done | bytes 8224 | tf_op jit(solution)/shard_map/ppermute | solution.py:524
  154.9 2.1 %finish.1 = f32[2048,256]{1,0:T(8,128)} custom-call(f32[2048,256]{1,0:T(8,128)S(1)} %get-tuple-element.82.d_ref.d0_ref, f32[2048,256]{1,0:T(8,128)S(1)} %get-tuple-element.100.d1_ref, f32[2048,1]{1,0:T(8,128)S(1)} %get-tuple-element.78.clamp_ref, f32[8,256]{1,0:T(8,128)S(1)} %get-tuple-element.101.step_ref, f32[8,256]{1,0:T(8,128)S(1)} %add_add_fusion.refs_0_, ...), custom_call_target="tpu_custom_call" | custom-call | flops 2097152 | bytes 6291456 | tf_op jit(solution)/shard_map/finish/pallas_call | solution.py:509
  (75 shorter events, 33.5 us)
Async XLA Ops:
  6.7 16.3 %collective-permute-start.3 = (f32[576,256]{1,0:T(8,128)S(1)}, f32[576,256]{1,0:T(8,128)S(1)}, u32[]{:S(2)}, u32[]{:S(2)}) collective-permute-start(f32[576,256]{1,0:T(8,128)S(1)} %get-tuple-element.62), channel_id=1, source_target_pairs={{0,8},{8,0},{16,24},{24,16},{1,9},{9,1},{17,25},{25,17},{2,10},{10... | collective-permute-start | bytes 1769480 | tf_op jit(solution)/shard_map/ppermute | solution.py:524
  9.7 10.6 %collective-permute-start.4 = (f32[288,256]{1,0:T(8,128)S(1)}, f32[288,256]{1,0:T(8,128)S(1)}, u32[]{:S(2)}, u32[]{:S(2)}) collective-permute-start(f32[288,256]{1,0:T(8,128)S(1)} %get-tuple-element.63), channel_id=1, source_target_pairs={{8,24},{16,0},{9,25},{17,1},{10,26},{18,2},{11,27},{19,3},{12,28},... | collective-permute-start | bytes 884744 | tf_op jit(solution)/shard_map/ppermute | solution.py:524
  15.4 17.7 %all-to-all-start = ((f32[8,96,128]{2,1,0:T(8,128)}), f32[8,96,128]{2,1,0:T(8,128)}, u32[]{:S(2)}, u32[]{:S(2)}) async-start(f32[8,96,128]{2,1,0:T(8,128)} %get-tuple-element.60), calls=%async_computation | async-start | bytes 786432 | tf_op jit(solution)/shard_map/all_to_all | solution.py:603
  23.0 13.9 %collective-permute-start.5 = (f32[576,256]{1,0:T(8,128)S(1)}, f32[576,256]{1,0:T(8,128)S(1)}, u32[]{:S(2)}, u32[]{:S(2)}) collective-permute-start(f32[576,256]{1,0:T(8,128)S(1)} %get-tuple-element.64), channel_id=1, source_target_pairs={{0,1},{1,0},{2,3},{3,2},{4,5},{5,4},{6,7},{7,6},{8,9},{9,8},{10,11... | collective-permute-start | bytes 1769480 | tf_op jit(solution)/shard_map/ppermute | solution.py:524
  23.0 14.0 %collective-permute-start.6 = (f32[576,256]{1,0:T(8,128)S(1)}, f32[576,256]{1,0:T(8,128)S(1)}, u32[]{:S(2)}, u32[]{:S(2)}) collective-permute-start(f32[576,256]{1,0:T(8,128)S(1)} %get-tuple-element.65), channel_id=1, source_target_pairs={{1,2},{2,1},{3,4},{4,3},{5,6},{6,5},{9,10},{10,9},{11,12},{12,11},... | collective-permute-start | bytes 1769480 | tf_op jit(solution)/shard_map/ppermute | solution.py:524
  24.5 19.0 %collective-permute-start.7 = (f32[288,256]{1,0:T(8,128)}, f32[288,256]{1,0:T(8,128)S(1)}, u32[]{:S(2)}, u32[]{:S(2)}) collective-permute-start(f32[288,256]{1,0:T(8,128)} %broadcast_select_fusion), channel_id=1, source_target_pairs={{0,8},{8,0},{16,24},{24,16},{1,9},{9,1},{17,25},{25,17},{2,10},{10... | collective-permute-start | bytes 884744 | tf_op jit(solution)/shard_map/ppermute | solution.py:524
  27.0 16.5 %collective-permute-start.8 = (f32[288,256]{1,0:T(8,128)}, f32[288,256]{1,0:T(8,128)}, u32[]{:S(2)}, u32[]{:S(2)}) collective-permute-start(f32[288,256]{1,0:T(8,128)} %slice.8), channel_id=1, source_target_pairs={{0,16},{24,8},{1,17},{25,9},{2,18},{26,10},{3,19},{27,11},{4,20},{... | collective-permute-start | bytes 884744 | tf_op jit(solution)/shard_map/ppermute | solution.py:524
  34.2 14.6 %collective-permute-start = (f32[2,96,128]{2,1,0:T(8,128)S(1)}, f32[2,96,128]{2,1,0:T(8,128)S(1)}, u32[]{:S(2)}, u32[]{:S(2)}) collective-permute-start(f32[2,96,128]{2,1,0:T(8,128)S(1)} %get-tuple-element.105), channel_id=1, source_target_pairs={{0,8},{8,0},{16,24},{24,16},{1,9},{9,1},{17,25},{25,17},{2,10},{10... | collective-permute-start | bytes 294920 | tf_op jit(solution)/shard_map/ppermute | solution.py:524
  36.9 11.9 %collective-permute-start.1 = (f32[2,96,128]{2,1,0:T(8,128)S(1)}, f32[2,96,128]{2,1,0:T(8,128)S(1)}, u32[]{:S(2)}, u32[]{:S(2)}) collective-permute-start(f32[2,96,128]{2,1,0:T(8,128)S(1)} %get-tuple-element.104), channel_id=1, source_target_pairs={{0,16},{8,24},{16,0},{24,8},{1,17},{9,25},{17,1},{25,9},{2,18},{10... | collective-permute-start | bytes 294920 | tf_op jit(solution)/shard_map/ppermute | solution.py:524
  37.0 11.8 %collective-permute-start.2 = (f32[2,96,128]{2,1,0:T(8,128)S(1)}, f32[2,96,128]{2,1,0:T(8,128)S(1)}, u32[]{:S(2)}, u32[]{:S(2)}) collective-permute-start(f32[2,96,128]{2,1,0:T(8,128)S(1)} %get-tuple-element.103), channel_id=1, source_target_pairs={{0,24},{8,16},{16,8},{24,0},{1,25},{9,17},{17,9},{25,1},{2,26},{10... | collective-permute-start | bytes 294920 | tf_op jit(solution)/shard_map/ppermute | solution.py:524
  48.8 5.0 %collective-permute-start.10 = (f32[32,256]{1,0:T(8,128)S(1)}, f32[32,256]{1,0:T(8,128)S(1)}, u32[]{:S(2)}, u32[]{:S(2)}) collective-permute-start(f32[32,256]{1,0:T(8,128)S(1)} %get-tuple-element.69.refs_4_), channel_id=1, source_target_pairs={{0,4},{1,5},{2,6},{3,7},{4,0},{5,1},{6,2},{7,3},{8,12},{9,13},{10,... | collective-permute-start | bytes 98312 | tf_op jit(solution)/shard_map/ppermute | solution.py:524
  51.4 5.7 %collective-permute-start.11 = (f32[32,256]{1,0:T(8,128)S(1)}, f32[32,256]{1,0:T(8,128)S(1)}, u32[]{:S(2)}, u32[]{:S(2)}) collective-permute-start(f32[32,256]{1,0:T(8,128)S(1)} %get-tuple-element.69.refs_4_), channel_id=1, source_target_pairs={{0,6},{1,7},{2,4},{3,5},{4,2},{5,3},{6,0},{7,1},{8,14},{9,15},{10,... | collective-permute-start | bytes 98312 | tf_op jit(solution)/shard_map/ppermute | solution.py:524
  52.2 4.9 %collective-permute-start.9 = (f32[32,256]{1,0:T(8,128)S(1)}, f32[32,256]{1,0:T(8,128)S(1)}, u32[]{:S(2)}, u32[]{:S(2)}) collective-permute-start(f32[32,256]{1,0:T(8,128)S(1)} %get-tuple-element.69.refs_4_), channel_id=1, source_target_pairs={{0,2},{1,3},{2,0},{3,1},{4,6},{5,7},{6,4},{7,5},{8,10},{9,11},{10,... | collective-permute-start | bytes 98312 | tf_op jit(solution)/shard_map/ppermute | solution.py:524
  59.5 13.5 %collective-permute-start.13 = (f32[160,256]{1,0:T(8,128)S(1)}, f32[160,256]{1,0:T(8,128)S(1)}, u32[]{:S(2)}, u32[]{:S(2)}) collective-permute-start(f32[160,256]{1,0:T(8,128)S(1)} %get-tuple-element.79), channel_id=1, source_target_pairs={{0,8},{8,0},{16,24},{24,16},{1,9},{9,1},{17,25},{25,17},{2,10},{10... | collective-permute-start | bytes 491528 | tf_op jit(solution)/shard_map/ppermute | solution.py:524
  62.2 10.8 %collective-permute-start.14 = (f32[160,256]{1,0:T(8,128)S(1)}, f32[160,256]{1,0:T(8,128)S(1)}, u32[]{:S(2)}, u32[]{:S(2)}) collective-permute-start(f32[160,256]{1,0:T(8,128)S(1)} %get-tuple-element.80), channel_id=1, source_target_pairs={{0,16},{8,24},{16,0},{24,8},{1,17},{9,25},{17,1},{25,9},{2,18},{10... | collective-permute-start | bytes 491528 | tf_op jit(solution)/shard_map/ppermute | solution.py:524
  62.3 10.7 %collective-permute-start.15 = (f32[160,256]{1,0:T(8,128)S(1)}, f32[160,256]{1,0:T(8,128)S(1)}, u32[]{:S(2)}, u32[]{:S(2)}) collective-permute-start(f32[160,256]{1,0:T(8,128)S(1)} %get-tuple-element.81), channel_id=1, source_target_pairs={{0,24},{8,16},{16,8},{24,0},{1,25},{9,17},{17,9},{25,1},{2,26},{10... | collective-permute-start | bytes 491528 | tf_op jit(solution)/shard_map/ppermute | solution.py:524
  82.6 10.0 %collective-permute-start.16 = (f32[256,256]{1,0:T(8,128)S(1)}, f32[256,256]{1,0:T(8,128)S(1)}, u32[]{:S(2)}, u32[]{:S(2)}) collective-permute-start(f32[256,256]{1,0:T(8,128)S(1)} %get-tuple-element.87), channel_id=1, source_target_pairs={{8,24},{16,0},{9,25},{17,1},{10,26},{18,2},{11,27},{19,3},{12,28},... | collective-permute-start | bytes 786440 | tf_op jit(solution)/shard_map/ppermute | solution.py:524
  84.1 15.1 %collective-permute-start.19 = (f32[512,256]{1,0:T(8,128)S(1)}, f32[512,256]{1,0:T(8,128)S(1)}, u32[]{:S(2)}, u32[]{:S(2)}) collective-permute-start(f32[512,256]{1,0:T(8,128)S(1)} %get-tuple-element.92), channel_id=1, source_target_pairs={{0,8},{8,0},{16,24},{24,16},{1,9},{9,1},{17,25},{25,17},{2,10},{10... | collective-permute-start | bytes 1572872 | tf_op jit(solution)/shard_map/ppermute | solution.py:524
  92.6 11.2 %collective-permute-start.17 = (f32[512,256]{1,0:T(8,128)S(1)}, f32[512,256]{1,0:T(8,128)S(1)}, u32[]{:S(2)}, u32[]{:S(2)}) collective-permute-start(f32[512,256]{1,0:T(8,128)S(1)} %get-tuple-element.90), channel_id=1, source_target_pairs={{0,1},{1,0},{2,3},{3,2},{4,5},{5,4},{6,7},{7,6},{8,9},{9,8},{10,11... | collective-permute-start | bytes 1572872 | tf_op jit(solution)/shard_map/ppermute | solution.py:524
  92.6 11.1 %collective-permute-start.18 = (f32[512,256]{1,0:T(8,128)S(1)}, f32[512,256]{1,0:T(8,128)S(1)}, u32[]{:S(2)}, u32[]{:S(2)}) collective-permute-start(f32[512,256]{1,0:T(8,128)S(1)} %get-tuple-element.91), channel_id=1, source_target_pairs={{1,2},{2,1},{3,4},{4,3},{5,6},{6,5},{9,10},{10,9},{11,12},{12,11},... | collective-permute-start | bytes 1572872 | tf_op jit(solution)/shard_map/ppermute | solution.py:524
  93.4 14.0 %collective-permute-start.20 = (f32[256,256]{1,0:T(8,128)S(1)}, f32[256,256]{1,0:T(8,128)S(1)}, u32[]{:S(2)}, u32[]{:S(2)}) collective-permute-start(f32[256,256]{1,0:T(8,128)S(1)} %broadcast_select_fusion.1), channel_id=1, source_target_pairs={{0,8},{8,0},{16,24},{24,16},{1,9},{9,1},{17,25},{25,17},{2,10},{10... | collective-permute-start | bytes 786440 | tf_op jit(solution)/shard_map/ppermute | solution.py:524
  99.2 8.4 %collective-permute-start.21 = (f32[256,256]{1,0:T(8,128)S(1)}, f32[256,256]{1,0:T(8,128)S(1)}, u32[]{:S(2)}, u32[]{:S(2)}) collective-permute-start(f32[256,256]{1,0:T(8,128)S(1)} %slice.9), channel_id=1, source_target_pairs={{0,16},{24,8},{1,17},{25,9},{2,18},{26,10},{3,19},{27,11},{4,20},{... | collective-permute-start | bytes 786440 | tf_op jit(solution)/shard_map/ppermute | solution.py:524
  111.9 4.5 %collective-permute-start.22 = (f32[40,256]{1,0:T(8,128)S(1)}, f32[40,256]{1,0:T(8,128)S(1)}, u32[]{:S(2)}, u32[]{:S(2)}) collective-permute-start(f32[40,256]{1,0:T(8,128)S(1)} %get-tuple-element.95.refs_4_), channel_id=1, source_target_pairs={{0,2},{1,3},{2,0},{3,1},{4,6},{5,7},{6,4},{7,5},{8,10},{9,11},{10,... | collective-permute-start | bytes 122888 | tf_op jit(solution)/shard_map/ppermute | solution.py:524
  111.9 5.8 %collective-permute-start.23 = (f32[40,256]{1,0:T(8,128)S(1)}, f32[40,256]{1,0:T(8,128)S(1)}, u32[]{:S(2)}, u32[]{:S(2)}) collective-permute-start(f32[40,256]{1,0:T(8,128)S(1)} %get-tuple-element.95.refs_4_), channel_id=1, source_target_pairs={{0,4},{1,5},{2,6},{3,7},{4,0},{5,1},{6,2},{7,3},{8,12},{9,13},{10,... | collective-permute-start | bytes 122888 | tf_op jit(solution)/shard_map/ppermute | solution.py:524
  114.5 5.8 %collective-permute-start.24 = (f32[40,256]{1,0:T(8,128)S(1)}, f32[40,256]{1,0:T(8,128)S(1)}, u32[]{:S(2)}, u32[]{:S(2)}) collective-permute-start(f32[40,256]{1,0:T(8,128)S(1)} %get-tuple-element.95.refs_4_), channel_id=1, source_target_pairs={{0,6},{1,7},{2,4},{3,5},{4,2},{5,3},{6,0},{7,1},{8,14},{9,15},{10,... | collective-permute-start | bytes 122888 | tf_op jit(solution)/shard_map/ppermute | solution.py:524
  122.7 7.7 %collective-permute-start.26 = (f32[168,256]{1,0:T(8,128)S(1)}, f32[168,256]{1,0:T(8,128)S(1)}, u32[]{:S(2)}, u32[]{:S(2)}) collective-permute-start(f32[168,256]{1,0:T(8,128)S(1)} %get-tuple-element.97), channel_id=1, source_target_pairs={{0,8},{8,0},{16,24},{24,16},{1,9},{9,1},{17,25},{25,17},{2,10},{10... | collective-permute-start | bytes 516104 | tf_op jit(solution)/shard_map/ppermute | solution.py:524
  125.3 9.8 %collective-permute-start.27 = (f32[168,256]{1,0:T(8,128)S(1)}, f32[168,256]{1,0:T(8,128)S(1)}, u32[]{:S(2)}, u32[]{:S(2)}) collective-permute-start(f32[168,256]{1,0:T(8,128)S(1)} %get-tuple-element.98), channel_id=1, source_target_pairs={{0,16},{8,24},{16,0},{24,8},{1,17},{9,25},{17,1},{25,9},{2,18},{10... | collective-permute-start | bytes 516104 | tf_op jit(solution)/shard_map/ppermute | solution.py:524
  125.4 9.8 %collective-permute-start.28 = (f32[168,256]{1,0:T(8,128)S(1)}, f32[168,256]{1,0:T(8,128)S(1)}, u32[]{:S(2)}, u32[]{:S(2)}) collective-permute-start(f32[168,256]{1,0:T(8,128)S(1)} %get-tuple-element.99), channel_id=1, source_target_pairs={{0,24},{8,16},{16,8},{24,0},{1,25},{9,17},{17,9},{25,1},{2,26},{10... | collective-permute-start | bytes 516104 | tf_op jit(solution)/shard_map/ppermute | solution.py:524
  141.4 4.5 %collective-permute-start.31 = (f32[8,256]{1,0:T(8,128)S(1)}, f32[8,256]{1,0:T(8,128)S(1)}, u32[]{:S(2)}, u32[]{:S(2)}) collective-permute-start(f32[8,256]{1,0:T(8,128)S(1)} %get-tuple-element.102), channel_id=1, source_target_pairs={{0,24},{8,16},{16,8},{24,0},{1,25},{9,17},{17,9},{25,1},{2,26},{10... | collective-permute-start | bytes 24584 | tf_op jit(solution)/shard_map/ppermute | solution.py:524
  145.9 4.4 %collective-permute-start.32 = (f32[8,256]{1,0:T(8,128)S(1)}, f32[8,256]{1,0:T(8,128)S(1)}, u32[]{:S(2)}, u32[]{:S(2)}) collective-permute-start(f32[8,256]{1,0:T(8,128)S(1)} %add_add_fusion.1), channel_id=1, source_target_pairs={{0,2},{1,3},{2,0},{3,1},{4,6},{5,7},{6,4},{7,5},{8,10},{9,11},{10,... | collective-permute-start | bytes 24584 | tf_op jit(solution)/shard_map/ppermute | solution.py:524
  145.9 4.6 %collective-permute-start.33 = (f32[8,256]{1,0:T(8,128)S(1)}, f32[8,256]{1,0:T(8,128)S(1)}, u32[]{:S(2)}, u32[]{:S(2)}) collective-permute-start(f32[8,256]{1,0:T(8,128)S(1)} %add_add_fusion.1), channel_id=1, source_target_pairs={{0,4},{1,5},{2,6},{3,7},{4,0},{5,1},{6,2},{7,3},{8,12},{9,13},{10,... | collective-permute-start | bytes 24584 | tf_op jit(solution)/shard_map/ppermute | solution.py:524
  148.3 5.4 %collective-permute-start.34 = (f32[8,256]{1,0:T(8,128)S(1)}, f32[8,256]{1,0:T(8,128)S(1)}, u32[]{:S(2)}, u32[]{:S(2)}) collective-permute-start(f32[8,256]{1,0:T(8,128)S(1)} %add_add_fusion.1), channel_id=1, source_target_pairs={{0,6},{1,7},{2,4},{3,5},{4,2},{5,3},{6,0},{7,1},{8,14},{9,15},{10,... | collective-permute-start | bytes 24584 | tf_op jit(solution)/shard_map/ppermute | solution.py:524
  (9 other events, 79.7 us)
where the time goes:
time: 157 us
  Pallas kernels  61.6 us (39%)
  starting transfers between devices  54.6 us (35%)
  waiting for transfers between devices  37.6 us (24%)
  local copies, waits for them, and re-layouts  1.83 us (1%)
    pallas_call x14, Pallas kernels, call(): pl.pallas_call(kernel, in_specs=in_specs, out_specs=[VMEM] * len(outs), o...  59.6 us
    ppermute x36, starting transfers between devices, send(): lax.ppermute(x, axis, [(i, j) for i, j in pairs if j is not None and 0 <=...  49.7 us
    ppermute x36, waiting for transfers between devices, send(): lax.ppermute(x, axis, [(i, j) for i, j in pairs if j is not None and 0 <=...  35.8 us
    all_to_all x1, starting transfers between devices, per_device(): lax.all_to_all(after(three, *col_sends), 'col', 0, 0, tiled=True)  4.89 us
  transfers between devices with their start and end apart: 37, of which 18 were waited for; matrix products, arithmetic and copies ran while one was open for 2% of the time, Pallas kernels for 21%

commit v1 on v0

--- a/solution.py
+++ b/solution.py
@@ -11,7 +11,7 @@
 BF16 = jnp.bfloat16
 PAD = 8
 GRANT = 8 * 1024 * 1024
-UNROLL = dict(add=1, extend=1, prepare=1, first=2, sums=2)
+UNROLL = dict(add=1, extend=1, prepare=1, first=4, sums=2)
 LIGHT = ("step_sums", "add")
 VMEM = pl.BlockSpec(memory_space=pltpu.VMEM)
 SMEM = pl.BlockSpec(memory_space=pltpu.SMEM)
@@ -195,6 +195,17 @@
     )
 
 
+def relay_kernel(place_ref, both_ref, other_ref, last_ref, pair_ref, far_ref):
+    tall = far_ref.shape[0]
+    pair_ref[...] = jnp.where(has_cross(place_ref[0], 4), last_ref[...], other_ref[...])
+    far_ref[...] = both_ref[:tall]
+
+
+def relay(place, both, other, last):
+    args = [place, *in_vmem([both, other, last])]
+    return call(relay_kernel, "relay", args, [SMEM] + [VMEM] * 3, [shaped(last.shape)] * 2, [], last.size)
+
+
 def faces_of(kinds, place_ref):
     return [(cross_face if cross else pair_face)(base, place_ref[base // 2]) for base, cross in kinds]
 
@@ -327,7 +338,7 @@
     copy.wait()
 
 
-def extend(groups, place, adj, rows, contact, op, modes, parts, tile=256):
+def extend(groups, place, adj, rows, contact, op, modes, parts, tile=512):
     order, count = op.shape[0], modes.shape[0]
     args = [place, adj, rows, contact, in_hbm(op), in_hbm(modes), *parts]
     w, column = shaped((order, 5 * count), BF16), shaped((order, 1))
@@ -532,18 +543,17 @@
     return i + 1 if i % 2 else i - 1
 
 
-def row_exchange(*sends):
+def row_exchange(place, *sends):
     size = lax.axis_size("row")
     if not splits(size):
         got = [swap(sends[0], "row", 1), send(sends[1], "row", other_side)]
         return got, got
     both, other, last = sends
-    tall = other.shape[0]
     both = swap(both, "row", 1)
     other = send(other, "row", lambda i: i ^ 2 if i in (1, 2) else None)
-    inner = has_cross(lax.axis_index("row"), size)
-    got_last = swap(jnp.where(inner, last, other), "row", 1)
-    got_other = send(both[:tall], "row", lambda i: i ^ 2 if i in (0, 3) else None)
+    to_pair, to_far = relay(place, both, other, last)
+    got_last = swap(to_pair, "row", 1)
+    got_other = send(to_far, "row", lambda i: i ^ 2 if i in (0, 3) else None)
     return [both, other], [both, got_last, got_other]
 
 
@@ -597,7 +607,7 @@
     place = jnp.stack([lax.axis_index("row"), lax.axis_index("col")]).astype(jnp.int32)
 
     *row_sends, x_parts, m_parts, rows, three = to_faces(0, place, rows, load, mode, coarse_inverse)
-    way, row_got = row_exchange(*row_sends)
+    way, row_got = row_exchange(place, *row_sends)
     col_sends = to_faces(2, place, rows, x_parts, m_parts)
     col_got = col_exchange(*after_all(col_sends, way))
     picked = by_row(lax.all_to_all(after(three, *col_sends), "col", 0, 0, tiled=True))
@@ -612,10 +622,10 @@
     d0, v = first(op, s0, w, clamp, amounts)
 
     *row_sends, x_parts = to_faces(0, place, rows, v)
-    way, row_got = row_exchange(*row_sends)
+    way, row_got = row_exchange(place, *row_sends)
     col_sends = to_faces(2, place, rows, x_parts)
-    sums = step_sums(op, d0, after(weight, *col_sends))
-    col_got = col_exchange(*after_all(col_sends, [*way[1:], sums]))
+    col_got = col_exchange(*after_all(col_sends, way[1:]))
+    sums = step_sums(op, d0, after(weight, col_got[0]))
     (part,) = add_faces(COLS, place, adj, rows, v, col_got)
     s1, coef = add_faces(ROWS, place, adj, rows, part, row_got, mode, sums)
     amounts, _ = coarse_amounts(place, inverse, coef, PAD)

time: 157 us -> 154 us (0.981)
    pallas_call x14 -> x16, Pallas kernels: 59.6 us -> 58.1 us  [call(): pl.pallas_call(kernel, in_specs=in_specs, out_specs=[VMEM] * len(outs), o...]
  transfers between devices with their start and end apart: 37 -> 37, of which waited for: 18 -> 20; matrix products, arithmetic and copies ran while one was open for 2% -> 1% of each run, Pallas kernels for 21% -> 21%
where the time goes in v1:
time: 154 us; the launch traced here: 153 us
  Pallas kernels  60.2 us (39%)
  starting transfers between devices  53.2 us (35%)
  waiting for transfers between devices  38.4 us (25%)
    pallas_call x16, Pallas kernels, call(): pl.pallas_call(kernel, in_specs=in_specs, out_specs=[VMEM] * len(outs), o...  58.1 us
    ppermute x36, starting transfers between devices, send(): lax.ppermute(x, axis, [(i, j) for i, j in pairs if j is not None and 0 <=...  48.3 us
    ppermute x36, waiting for transfers between devices, send(): lax.ppermute(x, axis, [(i, j) for i, j in pairs if j is not None and 0 <=...  36.3 us
    all_to_all x1, starting transfers between devices, per_device(): lax.all_to_all(after(three, *col_sends), 'col', 0, 0, tiled=True)  4.89 us
  transfers between devices with their start and end apart: 37, of which 20 were waited for; matrix products, arithmetic and copies ran while one was open for 1% of the time, Pallas kernels for 21%

profile of v1, /device:TPU:0, one launch (start us, length us, event | category | flops | bytes accessed | tf_op | source)
XLA Modules:
  0.0 153.3 jit_solution(8094095400442924250)
XLA Ops:
  0.1 6.6 %row_faces.2 = (f32[576,256]{1,0:T(8,128)S(1)}, f32[288,256]{1,0:T(8,128)S(1)}, f32[288,256]{1,0:T(8,128)S(1)}, bf16[2048,512]{1,0:T(8,128)(2,1)S(1)}, bf16[64,2...) custom-call(s32[2]{0:T(128)S(1)} %pad_add_fusion.place_ref, s32[4,512]{1,0:T(4,128)} %bitcast.22, ...), custom_call_target="tpu_custom_call" | custom-call | flops 2147483648 | bytes 2498568 | tf_op jit(solution)/shard_map/row_faces/pallas_call | solution.py:60
  6.7 3.0 %collective-permute-start.3 = (f32[576,256]{1,0:T(8,128)S(1)}, f32[576,256]{1,0:T(8,128)S(1)}, u32[]{:S(2)}, u32[]{:S(2)}) collective-permute-start(f32[576,256]{1,0:T(8,128)S(1)} %get-tuple-element.66), channel_id=1, source_target_pairs={{0,8},{8,0},{16,24},{24,16},{1,9},{9,1},{17,25},{25,17},{2,10},{10... | collective-permute-start | bytes 1769480 | tf_op jit(solution)/shard_map/ppermute | solution.py:535
  11.0 4.4 %col_faces.2 = (f32[576,256]{1,0:T(8,128)S(1)}, f32[576,256]{1,0:T(8,128)S(1)}) custom-call(s32[2]{0:T(128)S(1)} %pad_add_fusion.place_ref, s32[4,512]{1,0:T(4,128)S(1)} %get-tuple-element.59.refs_0_.rows_ref, bf16[2048,512]{1,0:T(8,128)(2,1)S(1)} %get-tuple-element.60.refs_1_, bf16[64,2048]{1,0:T(8,128)(2,1)S(1)} %get-tuple-element.61.refs_2_), custom_call_target="tpu_custom_call" | custom-call | flops 2147483648 | bytes 2367496 | tf_op jit(solution)/shard_map/col_faces/pallas_call | solution.py:60
  15.4 4.9 %all-to-all-start = ((f32[8,96,128]{2,1,0:T(8,128)}), f32[8,96,128]{2,1,0:T(8,128)}, u32[]{:S(2)}, u32[]{:S(2)}) async-start(f32[8,96,128]{2,1,0:T(8,128)} %get-tuple-element.64), calls=%async_computation | async-start | bytes 786432 | tf_op jit(solution)/shard_map/all_to_all | solution.py:613
  20.3 2.7 %collective-permute-done.3.both_ref.refs_1_ = f32[576,256]{1,0:T(8,128)S(1)} collective-permute-done((f32[576,256]{1,0:T(8,128)S(1)}, f32[576,256]{1,0:T(8,128)S(1)}, u32[]{:S(2)}, u32[]{:S(2)}) %collective-permute-start.3) | collective-permute-done | bytes 589856 | tf_op jit(solution)/shard_map/ppermute | solution.py:535
  26.9 4.2 %collective-permute-start.8 = (f32[288,256]{1,0:T(8,128)}, f32[288,256]{1,0:T(8,128)}, u32[]{:S(2)}, u32[]{:S(2)}) collective-permute-start(f32[288,256]{1,0:T(8,128)} %get-tuple-element.73), channel_id=1, source_target_pairs={{0,16},{24,8},{1,17},{25,9},{2,18},{26,10},{3,19},{27,11},{4,20},{... | collective-permute-start | bytes 884744 | tf_op jit(solution)/shard_map/ppermute | solution.py:535
  31.1 2.0 %all-to-all-done = f32[8,96,128]{2,1,0:T(8,128)} async-done(((f32[8,96,128]{2,1,0:T(8,128)}), f32[8,96,128]{2,1,0:T(8,128)}, u32[]{:S(2)}, u32[]{:S(2)}) %all-to-all-start) | async-done | bytes 393248 | tf_op jit(solution)/shard_map/all_to_all | solution.py:613
  34.2 2.7 %collective-permute-start = (f32[2,96,128]{2,1,0:T(8,128)S(1)}, f32[2,96,128]{2,1,0:T(8,128)S(1)}, u32[]{:S(2)}, u32[]{:S(2)}) collective-permute-start(f32[2,96,128]{2,1,0:T(8,128)S(1)} %get-tuple-element.113), channel_id=1, source_target_pairs={{0,8},{8,0},{16,24},{24,16},{1,9},{9,1},{17,25},{25,17},{2,10},{10... | collective-permute-start | bytes 294920 | tf_op jit(solution)/shard_map/ppermute | solution.py:535
  38.4 5.0 %add.50 = (f32[2048,256]{1,0:T(8,128)S(1)}, bf16[1024,128]{1,0:T(8,128)(2,1)S(1)}) custom-call(s32[2]{0:T(128)S(1)} %pad_add_fusion.place_ref, s32[4]{0:T(128)S(1)} %bitcast.14, s32[4,512]{1,0:T(4,128)S(1)} %get-tuple-element.59.refs_0_.rows_ref, f32[2048,256]{1,0:T(8,128)} %bitcast.21, f32[576,256]{1,0:T(8,128)S(1)} %collective-permute-done.5.refs_0_, ...), custom_call_target="tpu_custom_call" | custom-call | flops 21474836 | bytes 32850 | tf_op jit(solution)/shard_map/add/pallas_call | solution.py:60
  43.5 5.2 %last_add.2 = (f32[2048,256]{1,0:T(8,128)S(1)}, f32[32,256]{1,0:T(8,128)S(1)}, bf16[1024,128]{1,0:T(8,128)(2,1)S(1)}) custom-call(s32[2]{0:T(128)S(1)} %pad_add_fusion.place_ref, s32[4]{0:T(128)S(1)} %bitcast.15, s32[4,512]{1,0:T(4,128)S(1)} %get-tuple-element.59.refs_0_.rows_ref, ...), custom_call_target="tpu_custom_call", output_to_operand_aliasing={{0}: (3, {})} | custom-call | flops 2147483648 | bytes 3547160 | tf_op jit(solution)/shard_map/last_add/pallas_call | solution.py:60
  49.4 3.3 %collective-permute-start.10 = (f32[32,256]{1,0:T(8,128)S(1)}, f32[32,256]{1,0:T(8,128)S(1)}, u32[]{:S(2)}, u32[]{:S(2)}) collective-permute-start(f32[32,256]{1,0:T(8,128)S(1)} %get-tuple-element.75.refs_4_), channel_id=1, source_target_pairs={{0,4},{1,5},{2,6},{3,7},{4,0},{5,1},{6,2},{7,3},{8,12},{9,13},{10,... | collective-permute-start | bytes 98312 | tf_op jit(solution)/shard_map/ppermute | solution.py:535
  54.8 3.6 %collective-permute-done.11.refs_7_ = f32[32,256]{1,0:T(8,128)S(1)} collective-permute-done((f32[32,256]{1,0:T(8,128)S(1)}, f32[32,256]{1,0:T(8,128)S(1)}, u32[]{:S(2)}, u32[]{:S(2)}) %collective-permute-start.11) | collective-permute-done | bytes 32800 | tf_op jit(solution)/shard_map/ppermute | solution.py:535
  64.4 6.0 %extend.1 = (bf16[2048,160]{1,0:T(8,128)(2,1)S(1)}, bf16[2048,160]{1,0:T(8,128)(2,1)S(1)}, f32[2048,1]{1,0:T(8,128)S(1)}, f32[2048,1]{1,0:T(8,128)S(1)}, bf16[2048,2048]{1,0:T(8,128)(2,1)S(1)}) custom-call(s32[2]{0:T(128)S(1)} %pad_add_fusion.place_ref, s32[4]{0:T(128)S(1)} %bitcast.16, s32[4,512]{1,0:T(4,128)S(1)} %get-tuple-element.59.refs_0_.rows_ref, ...), custom_call_target="tpu_custom_call" | custom-call | flops 2147483648 | bytes 9191448 | tf_op jit(solution)/shard_map/extend/pallas_call | solution.py:60
  71.8 6.1 %first.1 = (f32[2048,256]{1,0:T(8,128)S(1)}, f32[2048,256]{1,0:T(8,128)S(1)}) custom-call(bf16[2048,2048]{1,0:T(8,128)(2,1)S(1)} %get-tuple-element.80.op_ref, f32[2048,256]{1,0:T(8,128)S(1)} %get-tuple-element.81.s_ref, bf16[2048,160]{1,0:T(8,128)(2,1)S(1)} %get-tuple-element.82.w_high, ...), custom_call_target="tpu_custom_call", output_to_operand_aliasing={{0}: (1, {})} | custom-call | flops 4294967296 | bytes 12460032 | tf_op jit(solution)/shard_map/first/pallas_call | solution.py:60
  77.9 3.2 %row_faces.3 = (f32[512,256]{1,0:T(8,128)S(1)}, f32[256,256]{1,0:T(8,128)S(1)}, f32[256,256]{1,0:T(8,128)S(1)}, bf16[2048,512]{1,0:T(8,128)(2,1)S(1)}) custom-call(s32[2]{0:T(128)S(1)} %pad_add_fusion.place_ref, s32[4,512]{1,0:T(4,128)S(1)} %get-tuple-element.59.refs_0_.rows_ref, f32[2048,256]{1,0:T(8,128)S(1)} %get-tuple-element.89.refs_1_.x_ref), custom_call_target="tpu_custom_call" | custom-call | flops 2147483648 | bytes 2105352 | tf_op jit(solution)/shard_map/row_faces/pallas_call | solution.py:60
  82.6 2.7 %collective-permute-start.19 = (f32[512,256]{1,0:T(8,128)S(1)}, f32[512,256]{1,0:T(8,128)S(1)}, u32[]{:S(2)}, u32[]{:S(2)}) collective-permute-start(f32[512,256]{1,0:T(8,128)S(1)} %get-tuple-element.98), channel_id=1, source_target_pairs={{0,8},{8,0},{16,24},{24,16},{1,9},{9,1},{17,25},{25,17},{2,10},{10... | collective-permute-start | bytes 1572872 | tf_op jit(solution)/shard_map/ppermute | solution.py:535
  85.3 3.0 %col_faces.3 = (f32[512,256]{1,0:T(8,128)S(1)}, f32[512,256]{1,0:T(8,128)S(1)}) custom-call(s32[2]{0:T(128)S(1)} %pad_add_fusion.place_ref, s32[4,512]{1,0:T(4,128)S(1)} %get-tuple-element.59.refs_0_.rows_ref, bf16[2048,512]{1,0:T(8,128)(2,1)S(1)} %get-tuple-element.90.refs_1_), custom_call_target="tpu_custom_call" | custom-call | flops 2147483648 | bytes 2105352 | tf_op jit(solution)/shard_map/col_faces/pallas_call | solution.py:60
  91.0 5.2 %collective-permute-done.19.both_ref.refs_2_ = f32[512,256]{1,0:T(8,128)S(1)} collective-permute-done((f32[512,256]{1,0:T(8,128)S(1)}, f32[512,256]{1,0:T(8,128)S(1)}, u32[]{:S(2)}, u32[]{:S(2)}) %collective-permute-start.19) | collective-permute-done | bytes 524320 | tf_op jit(solution)/shard_map/ppermute | solution.py:535
  98.6 2.2 %collective-permute-start.21 = (f32[256,256]{1,0:T(8,128)S(1)}, f32[256,256]{1,0:T(8,128)S(1)}, u32[]{:S(2)}, u32[]{:S(2)}) collective-permute-start(f32[256,256]{1,0:T(8,128)S(1)} %get-tuple-element.101), channel_id=1, source_target_pairs={{0,16},{24,8},{1,17},{25,9},{2,18},{26,10},{3,19},{27,11},{4,20},{... | collective-permute-start | bytes 786440 | tf_op jit(solution)/shard_map/ppermute | solution.py:535
  100.8 2.7 %step_sums.1.refs_1_ = f32[8,256]{1,0:T(8,128)S(1)} custom-call(bf16[2048,2048]{1,0:T(8,128)(2,1)S(1)} %get-tuple-element.80.op_ref, f32[2048,256]{1,0:T(8,128)S(1)} %get-tuple-element.88.d_ref.d0_ref, f32[2048,1]{1,0:T(8,128)S(1)} %get-tuple-element.97.weight_ref), custom_call_target="tpu_custom_call" | custom-call | flops 21474836 | bytes 104939 | tf_op jit(solution)/shard_map/step_sums/pallas_call | solution.py:60
  103.6 3.6 %add.51.x_ref = f32[2048,256]{1,0:T(8,128)S(1)} custom-call(s32[2]{0:T(128)S(1)} %pad_add_fusion.place_ref, s32[4]{0:T(128)S(1)} %bitcast.17, s32[4,512]{1,0:T(4,128)S(1)} %get-tuple-element.59.refs_0_.rows_ref, f32[2048,256]{1,0:T(8,128)S(1)} %get-tuple-element.89.refs_1_.x_ref, ...), custom_call_target="tpu_custom_call", output_to_operand_aliasing={{}: (3, {})} | custom-call | flops 21474836 | bytes 31539 | tf_op jit(solution)/shard_map/add/pallas_call | solution.py:60
  107.2 4.2 %last_add.3 = (f32[2048,256]{1,0:T(8,128)S(1)}, f32[40,256]{1,0:T(8,128)S(1)}) custom-call(s32[2]{0:T(128)S(1)} %pad_add_fusion.place_ref, s32[4]{0:T(128)S(1)} %bitcast.18, s32[4,512]{1,0:T(4,128)S(1)} %get-tuple-element.59.refs_0_.rows_ref, f32[2048,256]{1,0:T(8,128)S(1)} %add.51.x_ref, f32[32,2048]{1,0:T(8,128)S(1)} %bitcast.12, ...), custom_call_target="tpu_custom_call", output_to_operand_aliasing={{0}: (3, {})} | custom-call | flops 2147483648 | bytes 3424280 | tf_op jit(solution)/shard_map/last_add/pallas_call | solution.py:60
  111.6 2.1 %collective-permute-start.23 = (f32[40,256]{1,0:T(8,128)S(1)}, f32[40,256]{1,0:T(8,128)S(1)}, u32[]{:S(2)}, u32[]{:S(2)}) collective-permute-start(f32[40,256]{1,0:T(8,128)S(1)} %get-tuple-element.103.refs_4_), channel_id=1, source_target_pairs={{0,4},{1,5},{2,6},{3,7},{4,0},{5,1},{6,2},{7,3},{8,12},{9,13},{10,... | collective-permute-start | bytes 122888 | tf_op jit(solution)/shard_map/ppermute | solution.py:535
  113.7 2.1 %collective-permute-start.24 = (f32[40,256]{1,0:T(8,128)S(1)}, f32[40,256]{1,0:T(8,128)S(1)}, u32[]{:S(2)}, u32[]{:S(2)}) collective-permute-start(f32[40,256]{1,0:T(8,128)S(1)} %get-tuple-element.103.refs_4_), channel_id=1, source_target_pairs={{0,6},{1,7},{2,4},{3,5},{4,2},{5,3},{6,0},{7,1},{8,14},{9,15},{10,... | collective-permute-start | bytes 122888 | tf_op jit(solution)/shard_map/ppermute | solution.py:535
  116.5 3.0 %collective-permute-done.24.refs_7_ = f32[40,256]{1,0:T(8,128)S(1)} collective-permute-done((f32[40,256]{1,0:T(8,128)S(1)}, f32[40,256]{1,0:T(8,128)S(1)}, u32[]{:S(2)}, u32[]{:S(2)}) %collective-permute-start.24) | collective-permute-done | bytes 40992 | tf_op jit(solution)/shard_map/ppermute | solution.py:535
  122.1 2.0 %collective-permute-start.27 = (f32[168,256]{1,0:T(8,128)S(1)}, f32[168,256]{1,0:T(8,128)S(1)}, u32[]{:S(2)}, u32[]{:S(2)}) collective-permute-start(f32[168,256]{1,0:T(8,128)S(1)} %get-tuple-element.106), channel_id=1, source_target_pairs={{0,16},{8,24},{16,0},{24,8},{1,17},{9,25},{17,1},{25,9},{2,18},{10... | collective-permute-start | bytes 516104 | tf_op jit(solution)/shard_map/ppermute | solution.py:535
  125.5 3.7 %collective-permute-done.26.refs_1_ = f32[168,256]{1,0:T(8,128)S(1)} collective-permute-done((f32[168,256]{1,0:T(8,128)S(1)}, f32[168,256]{1,0:T(8,128)S(1)}, u32[]{:S(2)}, u32[]{:S(2)}) %collective-permute-start.26) | collective-permute-done | bytes 172064 | tf_op jit(solution)/shard_map/ppermute | solution.py:535
  129.2 3.0 %collective-permute-done.27.refs_2_ = f32[168,256]{1,0:T(8,128)S(1)} collective-permute-done((f32[168,256]{1,0:T(8,128)S(1)}, f32[168,256]{1,0:T(8,128)S(1)}, u32[]{:S(2)}, u32[]{:S(2)}) %collective-permute-start.27) | collective-permute-done | bytes 172064 | tf_op jit(solution)/shard_map/ppermute | solution.py:535
  132.2 4.2 %second.1 = (f32[2048,256]{1,0:T(8,128)S(1)}, f32[8,256]{1,0:T(8,128)S(1)}, f32[8,256]{1,0:T(8,128)S(1)}) custom-call(bf16[2048,2048]{1,0:T(8,128)(2,1)S(1)} %get-tuple-element.80.op_ref, f32[2048,256]{1,0:T(8,128)S(1)} %get-tuple-element.102.s_ref, f32[2048,256]{1,0:T(8,128)S(1)} %get-tuple-element.88.d_ref.d0_ref, ...), custom_call_target="tpu_custom_call", output_to_operand_aliasing={{0}: (1, {})} | custom-call | flops 2147483648 | bytes 14589952 | tf_op jit(solution)/shard_map/second/pallas_call | solution.py:60
  143.2 2.2 %collective-permute-start.34 = (f32[8,256]{1,0:T(8,128)S(1)}, f32[8,256]{1,0:T(8,128)S(1)}, u32[]{:S(2)}, u32[]{:S(2)}) collective-permute-start(f32[8,256]{1,0:T(8,128)S(1)} %add_add_fusion.1), channel_id=1, source_target_pairs={{0,6},{1,7},{2,4},{3,5},{4,2},{5,3},{6,0},{7,1},{8,14},{9,15},{10,... | collective-permute-start | bytes 24584 | tf_op jit(solution)/shard_map/ppermute | solution.py:535
  145.4 2.2 %collective-permute-start.32 = (f32[8,256]{1,0:T(8,128)S(1)}, f32[8,256]{1,0:T(8,128)S(1)}, u32[]{:S(2)}, u32[]{:S(2)}) collective-permute-start(f32[8,256]{1,0:T(8,128)S(1)} %add_add_fusion.1), channel_id=1, source_target_pairs={{0,2},{1,3},{2,0},{3,1},{4,6},{5,7},{6,4},{7,5},{8,10},{9,11},{10,... | collective-permute-start | bytes 24584 | tf_op jit(solution)/shard_map/ppermute | solution.py:535
  151.2 2.1 %finish.1 = f32[2048,256]{1,0:T(8,128)} custom-call(f32[2048,256]{1,0:T(8,128)S(1)} %get-tuple-element.88.d_ref.d0_ref, f32[2048,256]{1,0:T(8,128)S(1)} %get-tuple-element.108.d1_ref, f32[2048,1]{1,0:T(8,128)S(1)} %get-tuple-element.84.clamp_ref, f32[8,256]{1,0:T(8,128)S(1)} %get-tuple-element.109.step_ref, f32[8,256]{1,0:T(8,128)S(1)} %add_add_fusion.refs_0_, ...), custom_call_target="tpu_custom_call" | custom-call | flops 2097152 | bytes 6291456 | tf_op jit(solution)/shard_map/finish/pallas_call | solution.py:520
  (73 shorter events, 39.6 us)
Async XLA Ops:
  6.7 16.3 %collective-permute-start.3 = (f32[576,256]{1,0:T(8,128)S(1)}, f32[576,256]{1,0:T(8,128)S(1)}, u32[]{:S(2)}, u32[]{:S(2)}) collective-permute-start(f32[576,256]{1,0:T(8,128)S(1)} %get-tuple-element.66), channel_id=1, source_target_pairs={{0,8},{8,0},{16,24},{24,16},{1,9},{9,1},{17,25},{25,17},{2,10},{10... | collective-permute-start | bytes 1769480 | tf_op jit(solution)/shard_map/ppermute | solution.py:535
  9.7 10.6 %collective-permute-start.4 = (f32[288,256]{1,0:T(8,128)S(1)}, f32[288,256]{1,0:T(8,128)S(1)}, u32[]{:S(2)}, u32[]{:S(2)}) collective-permute-start(f32[288,256]{1,0:T(8,128)S(1)} %get-tuple-element.67), channel_id=1, source_target_pairs={{8,24},{16,0},{9,25},{17,1},{10,26},{18,2},{11,27},{19,3},{12,28},... | collective-permute-start | bytes 884744 | tf_op jit(solution)/shard_map/ppermute | solution.py:535
  15.4 17.7 %all-to-all-start = ((f32[8,96,128]{2,1,0:T(8,128)}), f32[8,96,128]{2,1,0:T(8,128)}, u32[]{:S(2)}, u32[]{:S(2)}) async-start(f32[8,96,128]{2,1,0:T(8,128)} %get-tuple-element.64), calls=%async_computation | async-start | bytes 786432 | tf_op jit(solution)/shard_map/all_to_all | solution.py:613
  23.0 13.9 %collective-permute-start.5 = (f32[576,256]{1,0:T(8,128)S(1)}, f32[576,256]{1,0:T(8,128)S(1)}, u32[]{:S(2)}, u32[]{:S(2)}) collective-permute-start(f32[576,256]{1,0:T(8,128)S(1)} %get-tuple-element.68), channel_id=1, source_target_pairs={{0,1},{1,0},{2,3},{3,2},{4,5},{5,4},{6,7},{7,6},{8,9},{9,8},{10,11... | collective-permute-start | bytes 1769480 | tf_op jit(solution)/shard_map/ppermute | solution.py:535
  23.0 14.0 %collective-permute-start.6 = (f32[576,256]{1,0:T(8,128)S(1)}, f32[576,256]{1,0:T(8,128)S(1)}, u32[]{:S(2)}, u32[]{:S(2)}) collective-permute-start(f32[576,256]{1,0:T(8,128)S(1)} %get-tuple-element.69), channel_id=1, source_target_pairs={{1,2},{2,1},{3,4},{4,3},{5,6},{6,5},{9,10},{10,9},{11,12},{12,11},... | collective-permute-start | bytes 1769480 | tf_op jit(solution)/shard_map/ppermute | solution.py:535
  25.2 18.3 %collective-permute-start.7 = (f32[288,256]{1,0:T(8,128)}, f32[288,256]{1,0:T(8,128)S(1)}, u32[]{:S(2)}, u32[]{:S(2)}) collective-permute-start(f32[288,256]{1,0:T(8,128)} %get-tuple-element.72), channel_id=1, source_target_pairs={{0,8},{8,0},{16,24},{24,16},{1,9},{9,1},{17,25},{25,17},{2,10},{10... | collective-permute-start | bytes 884744 | tf_op jit(solution)/shard_map/ppermute | solution.py:535
  26.9 16.6 %collective-permute-start.8 = (f32[288,256]{1,0:T(8,128)}, f32[288,256]{1,0:T(8,128)}, u32[]{:S(2)}, u32[]{:S(2)}) collective-permute-start(f32[288,256]{1,0:T(8,128)} %get-tuple-element.73), channel_id=1, source_target_pairs={{0,16},{24,8},{1,17},{25,9},{2,18},{26,10},{3,19},{27,11},{4,20},{... | collective-permute-start | bytes 884744 | tf_op jit(solution)/shard_map/ppermute | solution.py:535
  34.2 14.6 %collective-permute-start = (f32[2,96,128]{2,1,0:T(8,128)S(1)}, f32[2,96,128]{2,1,0:T(8,128)S(1)}, u32[]{:S(2)}, u32[]{:S(2)}) collective-permute-start(f32[2,96,128]{2,1,0:T(8,128)S(1)} %get-tuple-element.113), channel_id=1, source_target_pairs={{0,8},{8,0},{16,24},{24,16},{1,9},{9,1},{17,25},{25,17},{2,10},{10... | collective-permute-start | bytes 294920 | tf_op jit(solution)/shard_map/ppermute | solution.py:535
  36.9 11.9 %collective-permute-start.1 = (f32[2,96,128]{2,1,0:T(8,128)S(1)}, f32[2,96,128]{2,1,0:T(8,128)S(1)}, u32[]{:S(2)}, u32[]{:S(2)}) collective-permute-start(f32[2,96,128]{2,1,0:T(8,128)S(1)} %get-tuple-element.112), channel_id=1, source_target_pairs={{0,16},{8,24},{16,0},{24,8},{1,17},{9,25},{17,1},{25,9},{2,18},{10... | collective-permute-start | bytes 294920 | tf_op jit(solution)/shard_map/ppermute | solution.py:535
  37.0 11.8 %collective-permute-start.2 = (f32[2,96,128]{2,1,0:T(8,128)S(1)}, f32[2,96,128]{2,1,0:T(8,128)S(1)}, u32[]{:S(2)}, u32[]{:S(2)}) collective-permute-start(f32[2,96,128]{2,1,0:T(8,128)S(1)} %get-tuple-element.111), channel_id=1, source_target_pairs={{0,24},{8,16},{16,8},{24,0},{1,25},{9,17},{17,9},{25,1},{2,26},{10... | collective-permute-start | bytes 294920 | tf_op jit(solution)/shard_map/ppermute | solution.py:535
  48.8 4.5 %collective-permute-start.9 = (f32[32,256]{1,0:T(8,128)S(1)}, f32[32,256]{1,0:T(8,128)S(1)}, u32[]{:S(2)}, u32[]{:S(2)}) collective-permute-start(f32[32,256]{1,0:T(8,128)S(1)} %get-tuple-element.75.refs_4_), channel_id=1, source_target_pairs={{0,2},{1,3},{2,0},{3,1},{4,6},{5,7},{6,4},{7,5},{8,10},{9,11},{10,... | collective-permute-start | bytes 98312 | tf_op jit(solution)/shard_map/ppermute | solution.py:535
  49.4 5.4 %collective-permute-start.10 = (f32[32,256]{1,0:T(8,128)S(1)}, f32[32,256]{1,0:T(8,128)S(1)}, u32[]{:S(2)}, u32[]{:S(2)}) collective-permute-start(f32[32,256]{1,0:T(8,128)S(1)} %get-tuple-element.75.refs_4_), channel_id=1, source_target_pairs={{0,4},{1,5},{2,6},{3,7},{4,0},{5,1},{6,2},{7,3},{8,12},{9,13},{10,... | collective-permute-start | bytes 98312 | tf_op jit(solution)/shard_map/ppermute | solution.py:535
  52.7 5.7 %collective-permute-start.11 = (f32[32,256]{1,0:T(8,128)S(1)}, f32[32,256]{1,0:T(8,128)S(1)}, u32[]{:S(2)}, u32[]{:S(2)}) collective-permute-start(f32[32,256]{1,0:T(8,128)S(1)} %get-tuple-element.75.refs_4_), channel_id=1, source_target_pairs={{0,6},{1,7},{2,4},{3,5},{4,2},{5,3},{6,0},{7,1},{8,14},{9,15},{10,... | collective-permute-start | bytes 98312 | tf_op jit(solution)/shard_map/ppermute | solution.py:535
  60.8 9.6 %collective-permute-start.13 = (f32[160,256]{1,0:T(8,128)S(1)}, f32[160,256]{1,0:T(8,128)S(1)}, u32[]{:S(2)}, u32[]{:S(2)}) collective-permute-start(f32[160,256]{1,0:T(8,128)S(1)} %get-tuple-element.85), channel_id=1, source_target_pairs={{0,8},{8,0},{16,24},{24,16},{1,9},{9,1},{17,25},{25,17},{2,10},{10... | collective-permute-start | bytes 491528 | tf_op jit(solution)/shard_map/ppermute | solution.py:535
  62.3 9.5 %collective-permute-start.14 = (f32[160,256]{1,0:T(8,128)S(1)}, f32[160,256]{1,0:T(8,128)S(1)}, u32[]{:S(2)}, u32[]{:S(2)}) collective-permute-start(f32[160,256]{1,0:T(8,128)S(1)} %get-tuple-element.86), channel_id=1, source_target_pairs={{0,16},{8,24},{16,0},{24,8},{1,17},{9,25},{17,1},{25,9},{2,18},{10... | collective-permute-start | bytes 491528 | tf_op jit(solution)/shard_map/ppermute | solution.py:535
  62.4 9.4 %collective-permute-start.15 = (f32[160,256]{1,0:T(8,128)S(1)}, f32[160,256]{1,0:T(8,128)S(1)}, u32[]{:S(2)}, u32[]{:S(2)}) collective-permute-start(f32[160,256]{1,0:T(8,128)S(1)} %get-tuple-element.87), channel_id=1, source_target_pairs={{0,24},{8,16},{16,8},{24,0},{1,25},{9,17},{17,9},{25,1},{2,26},{10... | collective-permute-start | bytes 491528 | tf_op jit(solution)/shard_map/ppermute | solution.py:535
  81.1 9.2 %collective-permute-start.16 = (f32[256,256]{1,0:T(8,128)S(1)}, f32[256,256]{1,0:T(8,128)S(1)}, u32[]{:S(2)}, u32[]{:S(2)}) collective-permute-start(f32[256,256]{1,0:T(8,128)S(1)} %get-tuple-element.93), channel_id=1, source_target_pairs={{8,24},{16,0},{9,25},{17,1},{10,26},{18,2},{11,27},{19,3},{12,28},... | collective-permute-start | bytes 786440 | tf_op jit(solution)/shard_map/ppermute | solution.py:535
  82.6 13.6 %collective-permute-start.19 = (f32[512,256]{1,0:T(8,128)S(1)}, f32[512,256]{1,0:T(8,128)S(1)}, u32[]{:S(2)}, u32[]{:S(2)}) collective-permute-start(f32[512,256]{1,0:T(8,128)S(1)} %get-tuple-element.98), channel_id=1, source_target_pairs={{0,8},{8,0},{16,24},{24,16},{1,9},{9,1},{17,25},{25,17},{2,10},{10... | collective-permute-start | bytes 1572872 | tf_op jit(solution)/shard_map/ppermute | solution.py:535
  90.3 10.5 %collective-permute-start.17 = (f32[512,256]{1,0:T(8,128)S(1)}, f32[512,256]{1,0:T(8,128)S(1)}, u32[]{:S(2)}, u32[]{:S(2)}) collective-permute-start(f32[512,256]{1,0:T(8,128)S(1)} %get-tuple-element.94), channel_id=1, source_target_pairs={{0,1},{1,0},{2,3},{3,2},{4,5},{5,4},{6,7},{7,6},{8,9},{9,8},{10,11... | collective-permute-start | bytes 1572872 | tf_op jit(solution)/shard_map/ppermute | solution.py:535
  90.3 13.3 %collective-permute-start.18 = (f32[512,256]{1,0:T(8,128)S(1)}, f32[512,256]{1,0:T(8,128)S(1)}, u32[]{:S(2)}, u32[]{:S(2)}) collective-permute-start(f32[512,256]{1,0:T(8,128)S(1)} %get-tuple-element.95), channel_id=1, source_target_pairs={{1,2},{2,1},{3,4},{4,3},{5,6},{6,5},{9,10},{10,9},{11,12},{12,11},... | collective-permute-start | bytes 1572872 | tf_op jit(solution)/shard_map/ppermute | solution.py:535
  96.8 10.3 %collective-permute-start.20 = (f32[256,256]{1,0:T(8,128)S(1)}, f32[256,256]{1,0:T(8,128)S(1)}, u32[]{:S(2)}, u32[]{:S(2)}) collective-permute-start(f32[256,256]{1,0:T(8,128)S(1)} %get-tuple-element.100), channel_id=1, source_target_pairs={{0,8},{8,0},{16,24},{24,16},{1,9},{9,1},{17,25},{25,17},{2,10},{10... | collective-permute-start | bytes 786440 | tf_op jit(solution)/shard_map/ppermute | solution.py:535
  98.6 8.5 %collective-permute-start.21 = (f32[256,256]{1,0:T(8,128)S(1)}, f32[256,256]{1,0:T(8,128)S(1)}, u32[]{:S(2)}, u32[]{:S(2)}) collective-permute-start(f32[256,256]{1,0:T(8,128)S(1)} %get-tuple-element.101), channel_id=1, source_target_pairs={{0,16},{24,8},{1,17},{25,9},{2,18},{26,10},{3,19},{27,11},{4,20},{... | collective-permute-start | bytes 786440 | tf_op jit(solution)/shard_map/ppermute | solution.py:535
  111.4 4.5 %collective-permute-start.22 = (f32[40,256]{1,0:T(8,128)S(1)}, f32[40,256]{1,0:T(8,128)S(1)}, u32[]{:S(2)}, u32[]{:S(2)}) collective-permute-start(f32[40,256]{1,0:T(8,128)S(1)} %get-tuple-element.103.refs_4_), channel_id=1, source_target_pairs={{0,2},{1,3},{2,0},{3,1},{4,6},{5,7},{6,4},{7,5},{8,10},{9,11},{10,... | collective-permute-start | bytes 122888 | tf_op jit(solution)/shard_map/ppermute | solution.py:535
  111.6 4.9 %collective-permute-start.23 = (f32[40,256]{1,0:T(8,128)S(1)}, f32[40,256]{1,0:T(8,128)S(1)}, u32[]{:S(2)}, u32[]{:S(2)}) collective-permute-start(f32[40,256]{1,0:T(8,128)S(1)} %get-tuple-element.103.refs_4_), channel_id=1, source_target_pairs={{0,4},{1,5},{2,6},{3,7},{4,0},{5,1},{6,2},{7,3},{8,12},{9,13},{10,... | collective-permute-start | bytes 122888 | tf_op jit(solution)/shard_map/ppermute | solution.py:535
  113.7 5.8 %collective-permute-start.24 = (f32[40,256]{1,0:T(8,128)S(1)}, f32[40,256]{1,0:T(8,128)S(1)}, u32[]{:S(2)}, u32[]{:S(2)}) collective-permute-start(f32[40,256]{1,0:T(8,128)S(1)} %get-tuple-element.103.refs_4_), channel_id=1, source_target_pairs={{0,6},{1,7},{2,4},{3,5},{4,2},{5,3},{6,0},{7,1},{8,14},{9,15},{10,... | collective-permute-start | bytes 122888 | tf_op jit(solution)/shard_map/ppermute | solution.py:535
  122.0 7.3 %collective-permute-start.26 = (f32[168,256]{1,0:T(8,128)S(1)}, f32[168,256]{1,0:T(8,128)S(1)}, u32[]{:S(2)}, u32[]{:S(2)}) collective-permute-start(f32[168,256]{1,0:T(8,128)S(1)} %get-tuple-element.105), channel_id=1, source_target_pairs={{0,8},{8,0},{16,24},{24,16},{1,9},{9,1},{17,25},{25,17},{2,10},{10... | collective-permute-start | bytes 516104 | tf_op jit(solution)/shard_map/ppermute | solution.py:535
  122.1 10.1 %collective-permute-start.27 = (f32[168,256]{1,0:T(8,128)S(1)}, f32[168,256]{1,0:T(8,128)S(1)}, u32[]{:S(2)}, u32[]{:S(2)}) collective-permute-start(f32[168,256]{1,0:T(8,128)S(1)} %get-tuple-element.106), channel_id=1, source_target_pairs={{0,16},{8,24},{16,0},{24,8},{1,17},{9,25},{17,1},{25,9},{2,18},{10... | collective-permute-start | bytes 516104 | tf_op jit(solution)/shard_map/ppermute | solution.py:535
  124.1 8.1 %collective-permute-start.28 = (f32[168,256]{1,0:T(8,128)S(1)}, f32[168,256]{1,0:T(8,128)S(1)}, u32[]{:S(2)}, u32[]{:S(2)}) collective-permute-start(f32[168,256]{1,0:T(8,128)S(1)} %get-tuple-element.107), channel_id=1, source_target_pairs={{0,24},{8,16},{16,8},{24,0},{1,25},{9,17},{17,9},{25,1},{2,26},{10... | collective-permute-start | bytes 516104 | tf_op jit(solution)/shard_map/ppermute | solution.py:535
  136.4 4.6 %collective-permute-start.31 = (f32[8,256]{1,0:T(8,128)S(1)}, f32[8,256]{1,0:T(8,128)S(1)}, u32[]{:S(2)}, u32[]{:S(2)}) collective-permute-start(f32[8,256]{1,0:T(8,128)S(1)} %get-tuple-element.110), channel_id=1, source_target_pairs={{0,24},{8,16},{16,8},{24,0},{1,25},{9,17},{17,9},{25,1},{2,26},{10... | collective-permute-start | bytes 24584 | tf_op jit(solution)/shard_map/ppermute | solution.py:535
  143.2 5.4 %collective-permute-start.34 = (f32[8,256]{1,0:T(8,128)S(1)}, f32[8,256]{1,0:T(8,128)S(1)}, u32[]{:S(2)}, u32[]{:S(2)}) collective-permute-start(f32[8,256]{1,0:T(8,128)S(1)} %add_add_fusion.1), channel_id=1, source_target_pairs={{0,6},{1,7},{2,4},{3,5},{4,2},{5,3},{6,0},{7,1},{8,14},{9,15},{10,... | collective-permute-start | bytes 24584 | tf_op jit(solution)/shard_map/ppermute | solution.py:535
  145.4 4.5 %collective-permute-start.33 = (f32[8,256]{1,0:T(8,128)S(1)}, f32[8,256]{1,0:T(8,128)S(1)}, u32[]{:S(2)}, u32[]{:S(2)}) collective-permute-start(f32[8,256]{1,0:T(8,128)S(1)} %add_add_fusion.1), channel_id=1, source_target_pairs={{0,4},{1,5},{2,6},{3,7},{4,0},{5,1},{6,2},{7,3},{8,12},{9,13},{10,... | collective-permute-start | bytes 24584 | tf_op jit(solution)/shard_map/ppermute | solution.py:535
  145.4 4.5 %collective-permute-start.32 = (f32[8,256]{1,0:T(8,128)S(1)}, f32[8,256]{1,0:T(8,128)S(1)}, u32[]{:S(2)}, u32[]{:S(2)}) collective-permute-start(f32[8,256]{1,0:T(8,128)S(1)} %add_add_fusion.1), channel_id=1, source_target_pairs={{0,2},{1,3},{2,0},{3,1},{4,6},{5,7},{6,4},{7,5},{8,10},{9,11},{10,... | collective-permute-start | bytes 24584 | tf_op jit(solution)/shard_map/ppermute | solution.py:535
  (9 other events, 77.3 us)

commit v2 on v1

--- a/solution.py
+++ b/solution.py
@@ -11,7 +11,7 @@
 BF16 = jnp.bfloat16
 PAD = 8
 GRANT = 8 * 1024 * 1024
-UNROLL = dict(add=1, extend=1, prepare=1, first=4, sums=2)
+UNROLL = dict(add=2, extend=1, prepare=1, first=4, sums=4)
 LIGHT = ("step_sums", "add")
 VMEM = pl.BlockSpec(memory_space=pltpu.VMEM)
 SMEM = pl.BlockSpec(memory_space=pltpu.SMEM)
@@ -624,8 +624,8 @@
     *row_sends, x_parts = to_faces(0, place, rows, v)
     way, row_got = row_exchange(place, *row_sends)
     col_sends = to_faces(2, place, rows, x_parts)
-    col_got = col_exchange(*after_all(col_sends, way[1:]))
-    sums = step_sums(op, d0, after(weight, col_got[0]))
+    col_got = [swap(col_sends[0], "col", 1), send(after(col_sends[1], way[1]), "col", other_side)]
+    sums = step_sums(op, d0, after(weight, *way, col_got[0]))
     (part,) = add_faces(COLS, place, adj, rows, v, col_got)
     s1, coef = add_faces(ROWS, place, adj, rows, part, row_got, mode, sums)
     amounts, _ = coarse_amounts(place, inverse, coef, PAD)

time: 154 us -> 149 us (0.968)
  waiting for transfers between devices: 38.4 us -> 34.9 us
    ppermute x36, waiting for transfers between devices: 36.3 us -> 32.9 us  [send(): lax.ppermute(x, axis, [(i, j) for i, j in pairs if j is not None and 0 <=...]
  transfers between devices with their start and end apart: 37 -> 37, of which waited for: 20 -> 21; matrix products, arithmetic and copies ran while one was open for 1% -> 1% of each run, Pallas kernels for 21% -> 21%
where the time goes in v2:
time: 149 us
  Pallas kernels  59.1 us (40%)
  starting transfers between devices  53.4 us (36%)
  waiting for transfers between devices  34.9 us (23%)
    pallas_call x16, Pallas kernels, call(): pl.pallas_call(kernel, in_specs=in_specs, out_specs=[VMEM] * len(outs), o...  57.1 us
    ppermute x36, starting transfers between devices, send(): lax.ppermute(x, axis, [(i, j) for i, j in pairs if j is not None and 0 <=...  48.5 us
    ppermute x36, waiting for transfers between devices, send(): lax.ppermute(x, axis, [(i, j) for i, j in pairs if j is not None and 0 <=...  32.9 us
    all_to_all x1, starting transfers between devices, per_device(): lax.all_to_all(after(three, *col_sends), 'col', 0, 0, tiled=True)  4.89 us
  transfers between devices with their start and end apart: 37, of which 21 were waited for; matrix products, arithmetic and copies ran while one was open for 1% of the time, Pallas kernels for 21%

profile of v2, /device:TPU:0, one launch (start us, length us, event | category | flops | bytes accessed | tf_op | source)
XLA Modules:
  0.0 149.0 jit_solution(1141510384627971705)
XLA Ops:
  0.1 6.6 %row_faces.2 = (f32[576,256]{1,0:T(8,128)S(1)}, f32[288,256]{1,0:T(8,128)S(1)}, f32[288,256]{1,0:T(8,128)S(1)}, bf16[2048,512]{1,0:T(8,128)(2,1)S(1)}, bf16[64,2...) custom-call(s32[2]{0:T(128)S(1)} %pad_add_fusion.place_ref, s32[4,512]{1,0:T(4,128)} %bitcast.22, ...), custom_call_target="tpu_custom_call" | custom-call | flops 2147483648 | bytes 2498568 | tf_op jit(solution)/shard_map/row_faces/pallas_call | solution.py:60
  6.7 3.0 %collective-permute-start.3 = (f32[576,256]{1,0:T(8,128)S(1)}, f32[576,256]{1,0:T(8,128)S(1)}, u32[]{:S(2)}, u32[]{:S(2)}) collective-permute-start(f32[576,256]{1,0:T(8,128)S(1)} %get-tuple-element.65), channel_id=1, source_target_pairs={{0,8},{8,0},{16,24},{24,16},{1,9},{9,1},{17,25},{25,17},{2,10},{10... | collective-permute-start | bytes 1769480 | tf_op jit(solution)/shard_map/ppermute | solution.py:535
  11.0 4.4 %col_faces.2 = (f32[576,256]{1,0:T(8,128)S(1)}, f32[576,256]{1,0:T(8,128)S(1)}) custom-call(s32[2]{0:T(128)S(1)} %pad_add_fusion.place_ref, s32[4,512]{1,0:T(4,128)S(1)} %get-tuple-element.58.refs_0_.rows_ref, bf16[2048,512]{1,0:T(8,128)(2,1)S(1)} %get-tuple-element.59.refs_1_, bf16[64,2048]{1,0:T(8,128)(2,1)S(1)} %get-tuple-element.60.refs_2_), custom_call_target="tpu_custom_call" | custom-call | flops 2147483648 | bytes 2367496 | tf_op jit(solution)/shard_map/col_faces/pallas_call | solution.py:60
  15.4 4.9 %all-to-all-start = ((f32[8,96,128]{2,1,0:T(8,128)}), f32[8,96,128]{2,1,0:T(8,128)}, u32[]{:S(2)}, u32[]{:S(2)}) async-start(f32[8,96,128]{2,1,0:T(8,128)} %get-tuple-element.63), calls=%async_computation | async-start | bytes 786432 | tf_op jit(solution)/shard_map/all_to_all | solution.py:613
  20.3 2.7 %collective-permute-done.3.both_ref.refs_1_ = f32[576,256]{1,0:T(8,128)S(1)} collective-permute-done((f32[576,256]{1,0:T(8,128)S(1)}, f32[576,256]{1,0:T(8,128)S(1)}, u32[]{:S(2)}, u32[]{:S(2)}) %collective-permute-start.3) | collective-permute-done | bytes 589856 | tf_op jit(solution)/shard_map/ppermute | solution.py:535
  25.2 1.7 %collective-permute-start.7 = (f32[288,256]{1,0:T(8,128)}, f32[288,256]{1,0:T(8,128)S(1)}, u32[]{:S(2)}, u32[]{:S(2)}) collective-permute-start(f32[288,256]{1,0:T(8,128)} %get-tuple-element.71), channel_id=1, source_target_pairs={{0,8},{8,0},{16,24},{24,16},{1,9},{9,1},{17,25},{25,17},{2,10},{10... | collective-permute-start | bytes 884744 | tf_op jit(solution)/shard_map/ppermute | solution.py:535
  26.9 4.2 %collective-permute-start.8 = (f32[288,256]{1,0:T(8,128)}, f32[288,256]{1,0:T(8,128)}, u32[]{:S(2)}, u32[]{:S(2)}) collective-permute-start(f32[288,256]{1,0:T(8,128)} %get-tuple-element.72), channel_id=1, source_target_pairs={{0,16},{24,8},{1,17},{25,9},{2,18},{26,10},{3,19},{27,11},{4,20},{... | collective-permute-start | bytes 884744 | tf_op jit(solution)/shard_map/ppermute | solution.py:535
  31.1 2.0 %all-to-all-done = f32[8,96,128]{2,1,0:T(8,128)} async-done(((f32[8,96,128]{2,1,0:T(8,128)}), f32[8,96,128]{2,1,0:T(8,128)}, u32[]{:S(2)}, u32[]{:S(2)}) %all-to-all-start) | async-done | bytes 393248 | tf_op jit(solution)/shard_map/all_to_all | solution.py:613
  35.7 2.7 %collective-permute-start.1 = (f32[2,96,128]{2,1,0:T(8,128)S(1)}, f32[2,96,128]{2,1,0:T(8,128)S(1)}, u32[]{:S(2)}, u32[]{:S(2)}) collective-permute-start(f32[2,96,128]{2,1,0:T(8,128)S(1)} %get-tuple-element.110), channel_id=1, source_target_pairs={{0,16},{8,24},{16,0},{24,8},{1,17},{9,25},{17,1},{25,9},{2,18},{10... | collective-permute-start | bytes 294920 | tf_op jit(solution)/shard_map/ppermute | solution.py:535
  38.4 4.8 %add.50 = (f32[2048,256]{1,0:T(8,128)S(1)}, bf16[1024,128]{1,0:T(8,128)(2,1)S(1)}) custom-call(s32[2]{0:T(128)S(1)} %pad_add_fusion.place_ref, s32[4]{0:T(128)S(1)} %bitcast.14, s32[4,512]{1,0:T(4,128)S(1)} %get-tuple-element.58.refs_0_.rows_ref, f32[2048,256]{1,0:T(8,128)} %bitcast.21, f32[576,256]{1,0:T(8,128)S(1)} %collective-permute-done.5.refs_0_, ...), custom_call_target="tpu_custom_call" | custom-call | flops 21474836 | bytes 32850 | tf_op jit(solution)/shard_map/add/pallas_call | solution.py:60
  43.3 5.1 %last_add.2 = (f32[2048,256]{1,0:T(8,128)S(1)}, f32[32,256]{1,0:T(8,128)S(1)}, bf16[1024,128]{1,0:T(8,128)(2,1)S(1)}) custom-call(s32[2]{0:T(128)S(1)} %pad_add_fusion.place_ref, s32[4]{0:T(128)S(1)} %bitcast.15, s32[4,512]{1,0:T(4,128)S(1)} %get-tuple-element.58.refs_0_.rows_ref, ...), custom_call_target="tpu_custom_call", output_to_operand_aliasing={{0}: (3, {})} | custom-call | flops 2147483648 | bytes 3547160 | tf_op jit(solution)/shard_map/last_add/pallas_call | solution.py:60
  48.4 2.8 %collective-permute-start.11 = (f32[32,256]{1,0:T(8,128)S(1)}, f32[32,256]{1,0:T(8,128)S(1)}, u32[]{:S(2)}, u32[]{:S(2)}) collective-permute-start(f32[32,256]{1,0:T(8,128)S(1)} %get-tuple-element.74.refs_4_), channel_id=1, source_target_pairs={{0,6},{1,7},{2,4},{3,5},{4,2},{5,3},{6,0},{7,1},{8,14},{9,15},{10,... | collective-permute-start | bytes 98312 | tf_op jit(solution)/shard_map/ppermute | solution.py:535
  54.4 1.8 %collective-permute-done.10.refs_6_ = f32[32,256]{1,0:T(8,128)S(1)} collective-permute-done((f32[32,256]{1,0:T(8,128)S(1)}, f32[32,256]{1,0:T(8,128)S(1)}, u32[]{:S(2)}, u32[]{:S(2)}) %collective-permute-start.10) | collective-permute-done | bytes 32800 | tf_op jit(solution)/shard_map/ppermute | solution.py:535
  62.8 6.0 %extend.1 = (bf16[2048,160]{1,0:T(8,128)(2,1)S(1)}, bf16[2048,160]{1,0:T(8,128)(2,1)S(1)}, f32[2048,1]{1,0:T(8,128)S(1)}, f32[2048,1]{1,0:T(8,128)S(1)}, bf16[2048,2048]{1,0:T(8,128)(2,1)S(1)}) custom-call(s32[2]{0:T(128)S(1)} %pad_add_fusion.place_ref, s32[4]{0:T(128)S(1)} %bitcast.16, s32[4,512]{1,0:T(4,128)S(1)} %get-tuple-element.58.refs_0_.rows_ref, ...), custom_call_target="tpu_custom_call" | custom-call | flops 2147483648 | bytes 9191448 | tf_op jit(solution)/shard_map/extend/pallas_call | solution.py:60
  69.3 6.1 %first.1 = (f32[2048,256]{1,0:T(8,128)S(1)}, f32[2048,256]{1,0:T(8,128)S(1)}) custom-call(bf16[2048,2048]{1,0:T(8,128)(2,1)S(1)} %get-tuple-element.79.op_ref, f32[2048,256]{1,0:T(8,128)S(1)} %get-tuple-element.80.s_ref, bf16[2048,160]{1,0:T(8,128)(2,1)S(1)} %get-tuple-element.81.w_high, ...), custom_call_target="tpu_custom_call", output_to_operand_aliasing={{0}: (1, {})} | custom-call | flops 4294967296 | bytes 12460032 | tf_op jit(solution)/shard_map/first/pallas_call | solution.py:60
  75.4 3.2 %row_faces.3 = (f32[512,256]{1,0:T(8,128)S(1)}, f32[256,256]{1,0:T(8,128)S(1)}, f32[256,256]{1,0:T(8,128)S(1)}, bf16[2048,512]{1,0:T(8,128)(2,1)S(1)}) custom-call(s32[2]{0:T(128)S(1)} %pad_add_fusion.place_ref, s32[4,512]{1,0:T(4,128)S(1)} %get-tuple-element.58.refs_0_.rows_ref, f32[2048,256]{1,0:T(8,128)S(1)} %get-tuple-element.88.refs_1_.x_ref), custom_call_target="tpu_custom_call" | custom-call | flops 2147483648 | bytes 2105352 | tf_op jit(solution)/shard_map/row_faces/pallas_call | solution.py:60
  80.1 2.8 %collective-permute-start.19 = (f32[512,256]{1,0:T(8,128)S(1)}, f32[512,256]{1,0:T(8,128)S(1)}, u32[]{:S(2)}, u32[]{:S(2)}) collective-permute-start(f32[512,256]{1,0:T(8,128)S(1)} %get-tuple-element.95), channel_id=1, source_target_pairs={{0,8},{8,0},{16,24},{24,16},{1,9},{9,1},{17,25},{25,17},{2,10},{10... | collective-permute-start | bytes 1572872 | tf_op jit(solution)/shard_map/ppermute | solution.py:535
  82.9 3.0 %col_faces.3 = (f32[512,256]{1,0:T(8,128)S(1)}, f32[512,256]{1,0:T(8,128)S(1)}) custom-call(s32[2]{0:T(128)S(1)} %pad_add_fusion.place_ref, s32[4,512]{1,0:T(4,128)S(1)} %get-tuple-element.58.refs_0_.rows_ref, bf16[2048,512]{1,0:T(8,128)(2,1)S(1)} %get-tuple-element.89.refs_1_), custom_call_target="tpu_custom_call" | custom-call | flops 2147483648 | bytes 2105352 | tf_op jit(solution)/shard_map/col_faces/pallas_call | solution.py:60
  86.0 1.8 %collective-permute-done.17.other_ref = f32[256,256]{1,0:T(8,128)S(1)} collective-permute-done((f32[256,256]{1,0:T(8,128)S(1)}, f32[256,256]{1,0:T(8,128)S(1)}, u32[]{:S(2)}, u32[]{:S(2)}) %collective-permute-start.17) | collective-permute-done | bytes 262176 | tf_op jit(solution)/shard_map/ppermute | solution.py:535
  88.5 5.2 %collective-permute-done.19.both_ref.refs_2_ = f32[512,256]{1,0:T(8,128)S(1)} collective-permute-done((f32[512,256]{1,0:T(8,128)S(1)}, f32[512,256]{1,0:T(8,128)S(1)}, u32[]{:S(2)}, u32[]{:S(2)}) %collective-permute-start.19) | collective-permute-done | bytes 524320 | tf_op jit(solution)/shard_map/ppermute | solution.py:535
  94.3 1.8 %collective-permute-start.20 = (f32[256,256]{1,0:T(8,128)S(1)}, f32[256,256]{1,0:T(8,128)S(1)}, u32[]{:S(2)}, u32[]{:S(2)}) collective-permute-start(f32[256,256]{1,0:T(8,128)S(1)} %get-tuple-element.98), channel_id=1, source_target_pairs={{0,8},{8,0},{16,24},{24,16},{1,9},{9,1},{17,25},{25,17},{2,10},{10... | collective-permute-start | bytes 786440 | tf_op jit(solution)/shard_map/ppermute | solution.py:535
  96.1 2.3 %collective-permute-start.21 = (f32[256,256]{1,0:T(8,128)S(1)}, f32[256,256]{1,0:T(8,128)S(1)}, u32[]{:S(2)}, u32[]{:S(2)}) collective-permute-start(f32[256,256]{1,0:T(8,128)S(1)} %get-tuple-element.99), channel_id=1, source_target_pairs={{0,16},{24,8},{1,17},{25,9},{2,18},{26,10},{3,19},{27,11},{4,20},{... | collective-permute-start | bytes 786440 | tf_op jit(solution)/shard_map/ppermute | solution.py:535
  98.4 2.5 %step_sums.1.refs_1_ = f32[8,256]{1,0:T(8,128)S(1)} custom-call(bf16[2048,2048]{1,0:T(8,128)(2,1)S(1)} %get-tuple-element.79.op_ref, f32[2048,256]{1,0:T(8,128)S(1)} %get-tuple-element.87.d_ref.d0_ref, f32[2048,1]{1,0:T(8,128)S(1)} %get-tuple-element.96.weight_ref), custom_call_target="tpu_custom_call" | custom-call | flops 21474836 | bytes 104939 | tf_op jit(solution)/shard_map/step_sums/pallas_call | solution.py:60
  100.9 3.4 %add.51.x_ref = f32[2048,256]{1,0:T(8,128)S(1)} custom-call(s32[2]{0:T(128)S(1)} %pad_add_fusion.place_ref, s32[4]{0:T(128)S(1)} %bitcast.17, s32[4,512]{1,0:T(4,128)S(1)} %get-tuple-element.58.refs_0_.rows_ref, f32[2048,256]{1,0:T(8,128)S(1)} %get-tuple-element.88.refs_1_.x_ref, ...), custom_call_target="tpu_custom_call", output_to_operand_aliasing={{}: (3, {})} | custom-call | flops 21474836 | bytes 31539 | tf_op jit(solution)/shard_map/add/pallas_call | solution.py:60
  104.4 4.1 %last_add.3 = (f32[2048,256]{1,0:T(8,128)S(1)}, f32[40,256]{1,0:T(8,128)S(1)}) custom-call(s32[2]{0:T(128)S(1)} %pad_add_fusion.place_ref, s32[4]{0:T(128)S(1)} %bitcast.18, s32[4,512]{1,0:T(4,128)S(1)} %get-tuple-element.58.refs_0_.rows_ref, f32[2048,256]{1,0:T(8,128)S(1)} %add.51.x_ref, f32[32,2048]{1,0:T(8,128)S(1)} %bitcast.12, ...), custom_call_target="tpu_custom_call", output_to_operand_aliasing={{0}: (3, {})} | custom-call | flops 2147483648 | bytes 3424280 | tf_op jit(solution)/shard_map/last_add/pallas_call | solution.py:60
  108.4 2.1 %collective-permute-start.24 = (f32[40,256]{1,0:T(8,128)S(1)}, f32[40,256]{1,0:T(8,128)S(1)}, u32[]{:S(2)}, u32[]{:S(2)}) collective-permute-start(f32[40,256]{1,0:T(8,128)S(1)} %get-tuple-element.101.refs_4_), channel_id=1, source_target_pairs={{0,6},{1,7},{2,4},{3,5},{4,2},{5,3},{6,0},{7,1},{8,14},{9,15},{10,... | collective-permute-start | bytes 122888 | tf_op jit(solution)/shard_map/ppermute | solution.py:535
  121.7 3.7 %collective-permute-done.26.refs_1_ = f32[168,256]{1,0:T(8,128)S(1)} collective-permute-done((f32[168,256]{1,0:T(8,128)S(1)}, f32[168,256]{1,0:T(8,128)S(1)}, u32[]{:S(2)}, u32[]{:S(2)}) %collective-permute-start.26) | collective-permute-done | bytes 172064 | tf_op jit(solution)/shard_map/ppermute | solution.py:535
  125.4 3.0 %collective-permute-done.27.refs_2_ = f32[168,256]{1,0:T(8,128)S(1)} collective-permute-done((f32[168,256]{1,0:T(8,128)S(1)}, f32[168,256]{1,0:T(8,128)S(1)}, u32[]{:S(2)}, u32[]{:S(2)}) %collective-permute-start.27) | collective-permute-done | bytes 172064 | tf_op jit(solution)/shard_map/ppermute | solution.py:535
  128.4 4.0 %second.1 = (f32[2048,256]{1,0:T(8,128)S(1)}, f32[8,256]{1,0:T(8,128)S(1)}, f32[8,256]{1,0:T(8,128)S(1)}) custom-call(bf16[2048,2048]{1,0:T(8,128)(2,1)S(1)} %get-tuple-element.79.op_ref, f32[2048,256]{1,0:T(8,128)S(1)} %get-tuple-element.100.s_ref, f32[2048,256]{1,0:T(8,128)S(1)} %get-tuple-element.87.d_ref.d0_ref, ...), custom_call_target="tpu_custom_call", output_to_operand_aliasing={{0}: (1, {})} | custom-call | flops 2147483648 | bytes 14589952 | tf_op jit(solution)/shard_map/second/pallas_call | solution.py:60
  139.2 1.9 %collective-permute-start.34 = (f32[8,256]{1,0:T(8,128)S(1)}, f32[8,256]{1,0:T(8,128)S(1)}, u32[]{:S(2)}, u32[]{:S(2)}) collective-permute-start(f32[8,256]{1,0:T(8,128)S(1)} %add_add_fusion.1), channel_id=1, source_target_pairs={{0,6},{1,7},{2,4},{3,5},{4,2},{5,3},{6,0},{7,1},{8,14},{9,15},{10,... | collective-permute-start | bytes 24584 | tf_op jit(solution)/shard_map/ppermute | solution.py:535
  141.9 1.7 %collective-permute-start.32 = (f32[8,256]{1,0:T(8,128)S(1)}, f32[8,256]{1,0:T(8,128)S(1)}, u32[]{:S(2)}, u32[]{:S(2)}) collective-permute-start(f32[8,256]{1,0:T(8,128)S(1)} %add_add_fusion.1), channel_id=1, source_target_pairs={{0,2},{1,3},{2,0},{3,1},{4,6},{5,7},{6,4},{7,5},{8,10},{9,11},{10,... | collective-permute-start | bytes 24584 | tf_op jit(solution)/shard_map/ppermute | solution.py:535
  146.9 2.1 %finish.1 = f32[2048,256]{1,0:T(8,128)} custom-call(f32[2048,256]{1,0:T(8,128)S(1)} %get-tuple-element.87.d_ref.d0_ref, f32[2048,256]{1,0:T(8,128)S(1)} %get-tuple-element.106.d1_ref, f32[2048,1]{1,0:T(8,128)S(1)} %get-tuple-element.83.clamp_ref, f32[8,256]{1,0:T(8,128)S(1)} %get-tuple-element.107.step_ref, f32[8,256]{1,0:T(8,128)S(1)} %add_add_fusion.refs_0_, ...), custom_call_target="tpu_custom_call" | custom-call | flops 2097152 | bytes 6291456 | tf_op jit(solution)/shard_map/finish/pallas_call | solution.py:520
  (73 shorter events, 41.4 us)
Async XLA Ops:
  6.7 16.3 %collective-permute-start.3 = (f32[576,256]{1,0:T(8,128)S(1)}, f32[576,256]{1,0:T(8,128)S(1)}, u32[]{:S(2)}, u32[]{:S(2)}) collective-permute-start(f32[576,256]{1,0:T(8,128)S(1)} %get-tuple-element.65), channel_id=1, source_target_pairs={{0,8},{8,0},{16,24},{24,16},{1,9},{9,1},{17,25},{25,17},{2,10},{10... | collective-permute-start | bytes 1769480 | tf_op jit(solution)/shard_map/ppermute | solution.py:535
  9.7 10.6 %collective-permute-start.4 = (f32[288,256]{1,0:T(8,128)S(1)}, f32[288,256]{1,0:T(8,128)S(1)}, u32[]{:S(2)}, u32[]{:S(2)}) collective-permute-start(f32[288,256]{1,0:T(8,128)S(1)} %get-tuple-element.66), channel_id=1, source_target_pairs={{8,24},{16,0},{9,25},{17,1},{10,26},{18,2},{11,27},{19,3},{12,28},... | collective-permute-start | bytes 884744 | tf_op jit(solution)/shard_map/ppermute | solution.py:535
  15.4 17.7 %all-to-all-start = ((f32[8,96,128]{2,1,0:T(8,128)}), f32[8,96,128]{2,1,0:T(8,128)}, u32[]{:S(2)}, u32[]{:S(2)}) async-start(f32[8,96,128]{2,1,0:T(8,128)} %get-tuple-element.63), calls=%async_computation | async-start | bytes 786432 | tf_op jit(solution)/shard_map/all_to_all | solution.py:613
  23.0 12.6 %collective-permute-start.5 = (f32[576,256]{1,0:T(8,128)S(1)}, f32[576,256]{1,0:T(8,128)S(1)}, u32[]{:S(2)}, u32[]{:S(2)}) collective-permute-start(f32[576,256]{1,0:T(8,128)S(1)} %get-tuple-element.67), channel_id=1, source_target_pairs={{0,1},{1,0},{2,3},{3,2},{4,5},{5,4},{6,7},{7,6},{8,9},{9,8},{10,11... | collective-permute-start | bytes 1769480 | tf_op jit(solution)/shard_map/ppermute | solution.py:535
  23.0 15.3 %collective-permute-start.6 = (f32[576,256]{1,0:T(8,128)S(1)}, f32[576,256]{1,0:T(8,128)S(1)}, u32[]{:S(2)}, u32[]{:S(2)}) collective-permute-start(f32[576,256]{1,0:T(8,128)S(1)} %get-tuple-element.68), channel_id=1, source_target_pairs={{1,2},{2,1},{3,4},{4,3},{5,6},{6,5},{9,10},{10,9},{11,12},{12,11},... | collective-permute-start | bytes 1769480 | tf_op jit(solution)/shard_map/ppermute | solution.py:535
  25.2 18.1 %collective-permute-start.7 = (f32[288,256]{1,0:T(8,128)}, f32[288,256]{1,0:T(8,128)S(1)}, u32[]{:S(2)}, u32[]{:S(2)}) collective-permute-start(f32[288,256]{1,0:T(8,128)} %get-tuple-element.71), channel_id=1, source_target_pairs={{0,8},{8,0},{16,24},{24,16},{1,9},{9,1},{17,25},{25,17},{2,10},{10... | collective-permute-start | bytes 884744 | tf_op jit(solution)/shard_map/ppermute | solution.py:535
  26.9 16.4 %collective-permute-start.8 = (f32[288,256]{1,0:T(8,128)}, f32[288,256]{1,0:T(8,128)}, u32[]{:S(2)}, u32[]{:S(2)}) collective-permute-start(f32[288,256]{1,0:T(8,128)} %get-tuple-element.72), channel_id=1, source_target_pairs={{0,16},{24,8},{1,17},{25,9},{2,18},{26,10},{3,19},{27,11},{4,20},{... | collective-permute-start | bytes 884744 | tf_op jit(solution)/shard_map/ppermute | solution.py:535
  34.2 14.2 %collective-permute-start.2 = (f32[2,96,128]{2,1,0:T(8,128)S(1)}, f32[2,96,128]{2,1,0:T(8,128)S(1)}, u32[]{:S(2)}, u32[]{:S(2)}) collective-permute-start(f32[2,96,128]{2,1,0:T(8,128)S(1)} %get-tuple-element.109), channel_id=1, source_target_pairs={{0,24},{8,16},{16,8},{24,0},{1,25},{9,17},{17,9},{25,1},{2,26},{10... | collective-permute-start | bytes 294920 | tf_op jit(solution)/shard_map/ppermute | solution.py:535
  35.7 12.7 %collective-permute-start.1 = (f32[2,96,128]{2,1,0:T(8,128)S(1)}, f32[2,96,128]{2,1,0:T(8,128)S(1)}, u32[]{:S(2)}, u32[]{:S(2)}) collective-permute-start(f32[2,96,128]{2,1,0:T(8,128)S(1)} %get-tuple-element.110), channel_id=1, source_target_pairs={{0,16},{8,24},{16,0},{24,8},{1,17},{9,25},{17,1},{25,9},{2,18},{10... | collective-permute-start | bytes 294920 | tf_op jit(solution)/shard_map/ppermute | solution.py:535
  38.4 10.0 %collective-permute-start = (f32[2,96,128]{2,1,0:T(8,128)S(1)}, f32[2,96,128]{2,1,0:T(8,128)S(1)}, u32[]{:S(2)}, u32[]{:S(2)}) collective-permute-start(f32[2,96,128]{2,1,0:T(8,128)S(1)} %get-tuple-element.111), channel_id=1, source_target_pairs={{0,8},{8,0},{16,24},{24,16},{1,9},{9,1},{17,25},{25,17},{2,10},{10... | collective-permute-start | bytes 294920 | tf_op jit(solution)/shard_map/ppermute | solution.py:535
  48.4 6.0 %collective-permute-start.11 = (f32[32,256]{1,0:T(8,128)S(1)}, f32[32,256]{1,0:T(8,128)S(1)}, u32[]{:S(2)}, u32[]{:S(2)}) collective-permute-start(f32[32,256]{1,0:T(8,128)S(1)} %get-tuple-element.74.refs_4_), channel_id=1, source_target_pairs={{0,6},{1,7},{2,4},{3,5},{4,2},{5,3},{6,0},{7,1},{8,14},{9,15},{10,... | collective-permute-start | bytes 98312 | tf_op jit(solution)/shard_map/ppermute | solution.py:535
  51.2 4.9 %collective-permute-start.10 = (f32[32,256]{1,0:T(8,128)S(1)}, f32[32,256]{1,0:T(8,128)S(1)}, u32[]{:S(2)}, u32[]{:S(2)}) collective-permute-start(f32[32,256]{1,0:T(8,128)S(1)} %get-tuple-element.74.refs_4_), channel_id=1, source_target_pairs={{0,4},{1,5},{2,6},{3,7},{4,0},{5,1},{6,2},{7,3},{8,12},{9,13},{10,... | collective-permute-start | bytes 98312 | tf_op jit(solution)/shard_map/ppermute | solution.py:535
  52.3 4.5 %collective-permute-start.9 = (f32[32,256]{1,0:T(8,128)S(1)}, f32[32,256]{1,0:T(8,128)S(1)}, u32[]{:S(2)}, u32[]{:S(2)}) collective-permute-start(f32[32,256]{1,0:T(8,128)S(1)} %get-tuple-element.74.refs_4_), channel_id=1, source_target_pairs={{0,2},{1,3},{2,0},{3,1},{4,6},{5,7},{6,4},{7,5},{8,10},{9,11},{10,... | collective-permute-start | bytes 98312 | tf_op jit(solution)/shard_map/ppermute | solution.py:535
  59.2 9.6 %collective-permute-start.13 = (f32[160,256]{1,0:T(8,128)S(1)}, f32[160,256]{1,0:T(8,128)S(1)}, u32[]{:S(2)}, u32[]{:S(2)}) collective-permute-start(f32[160,256]{1,0:T(8,128)S(1)} %get-tuple-element.84), channel_id=1, source_target_pairs={{0,8},{8,0},{16,24},{24,16},{1,9},{9,1},{17,25},{25,17},{2,10},{10... | collective-permute-start | bytes 491528 | tf_op jit(solution)/shard_map/ppermute | solution.py:535
  59.8 9.5 %collective-permute-start.14 = (f32[160,256]{1,0:T(8,128)S(1)}, f32[160,256]{1,0:T(8,128)S(1)}, u32[]{:S(2)}, u32[]{:S(2)}) collective-permute-start(f32[160,256]{1,0:T(8,128)S(1)} %get-tuple-element.85), channel_id=1, source_target_pairs={{0,16},{8,24},{16,0},{24,8},{1,17},{9,25},{17,1},{25,9},{2,18},{10... | collective-permute-start | bytes 491528 | tf_op jit(solution)/shard_map/ppermute | solution.py:535
  61.3 8.0 %collective-permute-start.15 = (f32[160,256]{1,0:T(8,128)S(1)}, f32[160,256]{1,0:T(8,128)S(1)}, u32[]{:S(2)}, u32[]{:S(2)}) collective-permute-start(f32[160,256]{1,0:T(8,128)S(1)} %get-tuple-element.86), channel_id=1, source_target_pairs={{0,24},{8,16},{16,8},{24,0},{1,25},{9,17},{17,9},{25,1},{2,26},{10... | collective-permute-start | bytes 491528 | tf_op jit(solution)/shard_map/ppermute | solution.py:535
  78.6 9.2 %collective-permute-start.17 = (f32[256,256]{1,0:T(8,128)S(1)}, f32[256,256]{1,0:T(8,128)S(1)}, u32[]{:S(2)}, u32[]{:S(2)}) collective-permute-start(f32[256,256]{1,0:T(8,128)S(1)} %get-tuple-element.92), channel_id=1, source_target_pairs={{8,24},{16,0},{9,25},{17,1},{10,26},{18,2},{11,27},{19,3},{12,28},... | collective-permute-start | bytes 786440 | tf_op jit(solution)/shard_map/ppermute | solution.py:535
  80.1 13.6 %collective-permute-start.19 = (f32[512,256]{1,0:T(8,128)S(1)}, f32[512,256]{1,0:T(8,128)S(1)}, u32[]{:S(2)}, u32[]{:S(2)}) collective-permute-start(f32[512,256]{1,0:T(8,128)S(1)} %get-tuple-element.95), channel_id=1, source_target_pairs={{0,8},{8,0},{16,24},{24,16},{1,9},{9,1},{17,25},{25,17},{2,10},{10... | collective-permute-start | bytes 1572872 | tf_op jit(solution)/shard_map/ppermute | solution.py:535
  85.9 12.5 %collective-permute-start.16 = (f32[512,256]{1,0:T(8,128)S(1)}, f32[512,256]{1,0:T(8,128)S(1)}, u32[]{:S(2)}, u32[]{:S(2)}) collective-permute-start(f32[512,256]{1,0:T(8,128)S(1)} %get-tuple-element.90), channel_id=1, source_target_pairs={{0,1},{1,0},{2,3},{3,2},{4,5},{5,4},{6,7},{7,6},{8,9},{9,8},{10,11... | collective-permute-start | bytes 1572872 | tf_op jit(solution)/shard_map/ppermute | solution.py:535
  87.8 13.1 %collective-permute-start.18 = (f32[512,256]{1,0:T(8,128)S(1)}, f32[512,256]{1,0:T(8,128)S(1)}, u32[]{:S(2)}, u32[]{:S(2)}) collective-permute-start(f32[512,256]{1,0:T(8,128)S(1)} %get-tuple-element.93), channel_id=1, source_target_pairs={{1,2},{2,1},{3,4},{4,3},{5,6},{6,5},{9,10},{10,9},{11,12},{12,11},... | collective-permute-start | bytes 1572872 | tf_op jit(solution)/shard_map/ppermute | solution.py:535
  94.3 10.0 %collective-permute-start.20 = (f32[256,256]{1,0:T(8,128)S(1)}, f32[256,256]{1,0:T(8,128)S(1)}, u32[]{:S(2)}, u32[]{:S(2)}) collective-permute-start(f32[256,256]{1,0:T(8,128)S(1)} %get-tuple-element.98), channel_id=1, source_target_pairs={{0,8},{8,0},{16,24},{24,16},{1,9},{9,1},{17,25},{25,17},{2,10},{10... | collective-permute-start | bytes 786440 | tf_op jit(solution)/shard_map/ppermute | solution.py:535
  96.1 8.2 %collective-permute-start.21 = (f32[256,256]{1,0:T(8,128)S(1)}, f32[256,256]{1,0:T(8,128)S(1)}, u32[]{:S(2)}, u32[]{:S(2)}) collective-permute-start(f32[256,256]{1,0:T(8,128)S(1)} %get-tuple-element.99), channel_id=1, source_target_pairs={{0,16},{24,8},{1,17},{25,9},{2,18},{26,10},{3,19},{27,11},{4,20},{... | collective-permute-start | bytes 786440 | tf_op jit(solution)/shard_map/ppermute | solution.py:535
  108.4 5.9 %collective-permute-start.24 = (f32[40,256]{1,0:T(8,128)S(1)}, f32[40,256]{1,0:T(8,128)S(1)}, u32[]{:S(2)}, u32[]{:S(2)}) collective-permute-start(f32[40,256]{1,0:T(8,128)S(1)} %get-tuple-element.101.refs_4_), channel_id=1, source_target_pairs={{0,6},{1,7},{2,4},{3,5},{4,2},{5,3},{6,0},{7,1},{8,14},{9,15},{10,... | collective-permute-start | bytes 122888 | tf_op jit(solution)/shard_map/ppermute | solution.py:535
  110.5 5.2 %collective-permute-start.23 = (f32[40,256]{1,0:T(8,128)S(1)}, f32[40,256]{1,0:T(8,128)S(1)}, u32[]{:S(2)}, u32[]{:S(2)}) collective-permute-start(f32[40,256]{1,0:T(8,128)S(1)} %get-tuple-element.101.refs_4_), channel_id=1, source_target_pairs={{0,4},{1,5},{2,6},{3,7},{4,0},{5,1},{6,2},{7,3},{8,12},{9,13},{10,... | collective-permute-start | bytes 122888 | tf_op jit(solution)/shard_map/ppermute | solution.py:535
  111.3 4.4 %collective-permute-start.22 = (f32[40,256]{1,0:T(8,128)S(1)}, f32[40,256]{1,0:T(8,128)S(1)}, u32[]{:S(2)}, u32[]{:S(2)}) collective-permute-start(f32[40,256]{1,0:T(8,128)S(1)} %get-tuple-element.101.refs_4_), channel_id=1, source_target_pairs={{0,2},{1,3},{2,0},{3,1},{4,6},{5,7},{6,4},{7,5},{8,10},{9,11},{10,... | collective-permute-start | bytes 122888 | tf_op jit(solution)/shard_map/ppermute | solution.py:535
  118.1 7.3 %collective-permute-start.26 = (f32[168,256]{1,0:T(8,128)S(1)}, f32[168,256]{1,0:T(8,128)S(1)}, u32[]{:S(2)}, u32[]{:S(2)}) collective-permute-start(f32[168,256]{1,0:T(8,128)S(1)} %get-tuple-element.103), channel_id=1, source_target_pairs={{0,8},{8,0},{16,24},{24,16},{1,9},{9,1},{17,25},{25,17},{2,10},{10... | collective-permute-start | bytes 516104 | tf_op jit(solution)/shard_map/ppermute | solution.py:535
  118.5 9.9 %collective-permute-start.27 = (f32[168,256]{1,0:T(8,128)S(1)}, f32[168,256]{1,0:T(8,128)S(1)}, u32[]{:S(2)}, u32[]{:S(2)}) collective-permute-start(f32[168,256]{1,0:T(8,128)S(1)} %get-tuple-element.104), channel_id=1, source_target_pairs={{0,16},{8,24},{16,0},{24,8},{1,17},{9,25},{17,1},{25,9},{2,18},{10... | collective-permute-start | bytes 516104 | tf_op jit(solution)/shard_map/ppermute | solution.py:535
  120.2 8.2 %collective-permute-start.28 = (f32[168,256]{1,0:T(8,128)S(1)}, f32[168,256]{1,0:T(8,128)S(1)}, u32[]{:S(2)}, u32[]{:S(2)}) collective-permute-start(f32[168,256]{1,0:T(8,128)S(1)} %get-tuple-element.105), channel_id=1, source_target_pairs={{0,24},{8,16},{16,8},{24,0},{1,25},{9,17},{17,9},{25,1},{2,26},{10... | collective-permute-start | bytes 516104 | tf_op jit(solution)/shard_map/ppermute | solution.py:535
  132.4 4.6 %collective-permute-start.31 = (f32[8,256]{1,0:T(8,128)S(1)}, f32[8,256]{1,0:T(8,128)S(1)}, u32[]{:S(2)}, u32[]{:S(2)}) collective-permute-start(f32[8,256]{1,0:T(8,128)S(1)} %get-tuple-element.108), channel_id=1, source_target_pairs={{0,24},{8,16},{16,8},{24,0},{1,25},{9,17},{17,9},{25,1},{2,26},{10... | collective-permute-start | bytes 24584 | tf_op jit(solution)/shard_map/ppermute | solution.py:535
  139.2 5.4 %collective-permute-start.34 = (f32[8,256]{1,0:T(8,128)S(1)}, f32[8,256]{1,0:T(8,128)S(1)}, u32[]{:S(2)}, u32[]{:S(2)}) collective-permute-start(f32[8,256]{1,0:T(8,128)S(1)} %add_add_fusion.1), channel_id=1, source_target_pairs={{0,6},{1,7},{2,4},{3,5},{4,2},{5,3},{6,0},{7,1},{8,14},{9,15},{10,... | collective-permute-start | bytes 24584 | tf_op jit(solution)/shard_map/ppermute | solution.py:535
  141.1 4.5 %collective-permute-start.33 = (f32[8,256]{1,0:T(8,128)S(1)}, f32[8,256]{1,0:T(8,128)S(1)}, u32[]{:S(2)}, u32[]{:S(2)}) collective-permute-start(f32[8,256]{1,0:T(8,128)S(1)} %add_add_fusion.1), channel_id=1, source_target_pairs={{0,4},{1,5},{2,6},{3,7},{4,0},{5,1},{6,2},{7,3},{8,12},{9,13},{10,... | collective-permute-start | bytes 24584 | tf_op jit(solution)/shard_map/ppermute | solution.py:535
  141.9 3.8 %collective-permute-start.32 = (f32[8,256]{1,0:T(8,128)S(1)}, f32[8,256]{1,0:T(8,128)S(1)}, u32[]{:S(2)}, u32[]{:S(2)}) collective-permute-start(f32[8,256]{1,0:T(8,128)S(1)} %add_add_fusion.1), channel_id=1, source_target_pairs={{0,2},{1,3},{2,0},{3,1},{4,6},{5,7},{6,4},{7,5},{8,10},{9,11},{10,... | collective-permute-start | bytes 24584 | tf_op jit(solution)/shard_map/ppermute | solution.py:535
  (9 other events, 75.5 us)
